TPU v7x, 128 devices: a whole 4x4x4 slice. The times are simulated.
128 devices in a mesh: dp: 2 (over z_lo), ctx: 8 (over x, core), exp: 8 (over y, z_hi).
Axes of the slice: x: 4, y: 4, z: 4 (z_hi: 2, z_lo: 2; z = z_hi * 2 + z_lo), core: 2. Of those that a mesh axis runs over, the one named last changes fastest.
Arguments:
- queries: bfloat16 [6144, 8192], P(('dp', 'ctx'), 'exp'), parts along dimension 0, may hold values from -140 to 140
- keys: bfloat16 [6144, 512], P(('dp', 'ctx')), parts along dimension 0, may hold values from -4.5 to 4.5
- values: bfloat16 [6144, 512], P(('dp', 'ctx')), parts along dimension 0, may hold values from -5 to 5
- offsets: int32 [16], P('dp'), parts along dimension 0, may hold values from 0 to 2688, as said below
- out_proj: bfloat16 [8192, 4096], P('exp', 'ctx'), may hold values from -0.0625 to 0.0625
- residual: bfloat16 [6144, 4096], P(('dp', 'ctx', 'exp')), parts along dimension 0, may hold values from -12 to 12
- norm_gain: float32 [4096], replicated, may hold values from 0.1 to 1.9
- expert_ids: int32 [6144, 8], P(('dp', 'ctx', 'exp')), parts along dimension 0, may hold values from 0 to 63, all different within a row; in each aligned block of 48 rows (0 to 47, 48 to 95, ...) at most 12 rows name the same one
- gate_probs: float32 [6144, 8], P(('dp', 'ctx', 'exp')), parts along dimension 0, may hold values from 0.05 to 0.3
- w_gate: bfloat16 [64, 4096, 768], P(('ctx', 'exp')), may hold values from -0.09375 to 0.09375
- w_up: bfloat16 [64, 4096, 768], P(('ctx', 'exp')), may hold values from -0.09375 to 0.09375
- w_down: bfloat16 [64, 768, 4096], P(('ctx', 'exp')), may hold values from -0.21875 to 0.21875
Outputs:
- output: bfloat16 [6144, 4096], P(('dp', 'ctx', 'exp')), parts along dimension 0
There are 2 independent parts, one for each index of `dp`. A program takes and returns all parts, laid end to end along the dimension named above; an argument that names none is the same for every part. Nothing has to cross between parts.
Inputs may be any that keep to these rules, and one draw needn't show every extreme that they name: A permutation of 0, 384, ..., 2688: span c holds the tokens at window positions offsets[c] to offsets[c] + 383. `expert_ids`: each row names 8 different experts; within the rows of one device (aligned blocks of 48 rows) no expert is named by more than 12 rows, a bound that some block reaches.
All inputs are finite; a program needn't handle non-finite values.
Results may differ from a plain program's by a relative error of at most 0.017.
Values may be sent and summed in bfloat16 or wider, within the bound.
A program may use at most 192 MiB of HBM per device.

v0:
```python
import jax
import jax.numpy as jnp
from jax import lax
from jax.sharding import PartitionSpec as P

HQ = 64
KVH = 4
HD = 128


NEG_FILL = -1e30


def span_positions(offsets, owners, within):
    slot_ids = lax.iota(jnp.int32, offsets.shape[0])
    table = jnp.where(owners[:, None] == slot_ids[None, :], offsets[None, :], 0)
    return jnp.sum(table, axis=1) + within


def fold_update(carry, key_piece, value_piece, query_block, query_pos, key_pos):
    run_max, run_sum, run_acc = carry
    visible = key_pos[None, :] <= query_pos[:, None]
    scores = jnp.einsum(
        "qhd,kd->hqk", query_block, key_piece, preferred_element_type=jnp.float32
    ) * HD ** (-0.5)
    scores = jnp.where(visible[None], scores, NEG_FILL)
    new_max = jnp.maximum(run_max, jnp.max(scores, axis=2))
    weights = jnp.where(visible[None], jnp.exp(scores - new_max[:, :, None]), 0.0)
    new_sum = jnp.sum(weights, axis=2)
    mixed = jnp.einsum(
        "hqk,kd->hqd", weights.astype(jnp.bfloat16), value_piece, preferred_element_type=jnp.float32
    )
    return (new_max, new_sum, mixed)


def shards(
    queries,
    keys,
    values,
    offsets,
    out_proj,
    residual,
    norm_gain,
    expert_ids,
    gate_probs,
    w_gate,
    w_up,
    w_down,
):
    span = queries.shape[0]
    heads_here = queries.shape[1] // HD
    group_size = HQ // KVH
    ctx_place = lax.axis_index("ctx")
    exp_place = lax.axis_index("exp")
    kv_head = exp_place * heads_here // group_size
    key_head = lax.dynamic_slice_in_dim(keys, kv_head * HD, HD, 1)
    value_head = lax.dynamic_slice_in_dim(values, kv_head * HD, HD, 1)
    own_index = lax.iota(jnp.int32, span)
    query_pos = span_positions(offsets, jnp.zeros((span,), jnp.int32) + ctx_place, own_index)
    query_block = queries.reshape(span, heads_here, HD)
    start_state = (
        jnp.full((heads_here, span), NEG_FILL, jnp.float32),
        jnp.zeros((heads_here, span), jnp.float32),
        jnp.zeros((heads_here, span, HD), jnp.float32),
    )
    key_piece = lax.all_gather(key_head, "ctx", axis=0, tiled=True)
    value_piece = lax.all_gather(value_head, "ctx", axis=0, tiled=True)
    count = key_piece.shape[0]
    key_index = lax.iota(jnp.int32, count)
    key_pos = span_positions(offsets, key_index // span, key_index % span)
    final_max, final_sum, final_acc = fold_update(
        start_state, key_piece, value_piece, query_block, query_pos, key_pos
    )
    attention = (
        jnp.transpose(final_acc / final_sum[:, :, None], (1, 0, 2))
        .reshape(span, heads_here * HD)
        .astype(jnp.bfloat16)
    )
    partial_sum = jnp.dot(
        attention,
        lax.all_gather(out_proj, "ctx", axis=1, tiled=True),
        preferred_element_type=jnp.float32,
    )
    rounded = lax.optimization_barrier(partial_sum.astype(jnp.bfloat16)).astype(jnp.float32)
    attn_sum = lax.psum_scatter(
        rounded.astype(jnp.bfloat16), "exp", scatter_dimension=0, tiled=True
    ).astype(jnp.float32)
    hidden = residual.astype(jnp.float32) + attn_sum
    inverse = lax.rsqrt(jnp.mean(hidden * hidden, axis=1, keepdims=True) + 1e-06)
    normed = (hidden * inverse * norm_gain[None, :]).astype(jnp.bfloat16)
    token_rows = normed.shape[0]
    width = normed.shape[1]
    top_count = expert_ids.shape[1]
    ctx_count = lax.axis_size("ctx")
    exp_count = lax.axis_size("exp")
    expert_count = ctx_count * exp_count
    capacity = 2 * token_rows * top_count // expert_count
    flat_ids = expert_ids.reshape(-1)
    one_hot = (flat_ids[:, None] == lax.iota(jnp.int32, expert_count)[None, :]).astype(jnp.int32)
    earlier = jnp.cumsum(one_hot, axis=0) - one_hot
    ranks = jnp.sum(earlier * one_hot, axis=1)
    owner_rows = lax.iota(jnp.int32, token_rows * top_count) // top_count
    table = (
        jnp.full((expert_count, capacity), token_rows, jnp.int32)
        .at[flat_ids, ranks]
        .set(owner_rows)
    )
    padded = jnp.concatenate([normed, jnp.zeros((1, width), jnp.bfloat16)], axis=0)
    outgoing = padded[table]
    arrived = lax.all_to_all(outgoing, ("ctx", "exp"), split_axis=0, concat_axis=0, tiled=True)
    flat_rows = arrived.reshape(-1, width)
    gate_proj = jnp.dot(flat_rows, w_gate[0], preferred_element_type=jnp.float32)
    up_proj = jnp.dot(flat_rows, w_up[0], preferred_element_type=jnp.float32)
    activated = (jax.nn.silu(gate_proj) * up_proj).astype(jnp.bfloat16)
    produced = jnp.dot(activated, w_down[0], preferred_element_type=jnp.float32).astype(
        jnp.bfloat16
    )
    returned = lax.all_to_all(
        produced.reshape(arrived.shape), ("ctx", "exp"), split_axis=0, concat_axis=0, tiled=True
    )
    picked = returned[flat_ids, ranks].reshape(token_rows, top_count, width)
    mixture = jnp.sum(gate_probs[:, :, None] * picked.astype(jnp.float32), axis=1)
    return (hidden + mixture).astype(jnp.bfloat16)


def solution(mesh):
    return jax.shard_map(
        shards,
        mesh=mesh,
        in_specs=(
            P(("dp", "ctx"), "exp"),
            P(("dp", "ctx"), None),
            P(("dp", "ctx"), None),
            P("dp"),
            P("exp", "ctx"),
            P(("dp", "ctx", "exp"), None),
            P(),
            P(("dp", "ctx", "exp"), None),
            P(("dp", "ctx", "exp"), None),
            P(("ctx", "exp"), None, None),
            P(("ctx", "exp"), None, None),
            P(("ctx", "exp"), None, None),
        ),
        out_specs=P(("dp", "ctx", "exp"), None),
        check_vma=False,
    )
```

profile of v0, /device:TPU:1, one launch (start us, length us, event | category | flops | bytes accessed | tf_op | source)
XLA Modules:
  0.0 498.5 jit_solution(1980622138200535442)
XLA Ops:
  6.5 0.0 all-gather.2.cloned.1.call-start
  6.5 0.7 all-gather.2.cloned.1.call-update
  7.3 0.0 reduce-scatter.2.cloned.1.call-start
  7.3 0.9 constant_dynamic-slice_fusion
  8.2 0.1 copy.49
  8.4 0.9 constant_dynamic-slice_fusion.1
  9.3 0.8 select_reduce_fusion
  10.1 0.7 select_reduce_fusion.1
  10.8 15.1 %all_gather.9 = bf16[3072,128]{1,0:T(8,128)(2,1)S(1)} all-gather(bf16[384,128]{1,0:T(8,128)(2,1)S(1)} %constant_dynamic-slice_fusion.1), channel_id=1, replica_groups=mesh['dp'=2,'ctx'=8,'exp'=8] {'ctx'}, dimensions={0}, use_global_device_ids=true | all-gather | bytes 884736 | tf_op jit(solution)/shard_map/all_gather | solution.py:66
  25.9 1.4 broadcast_compare_fusion
  27.3 14.6 %fusion = (f32[8,384]{1,0:T(8,128)S(1)}, f32[3072,384,8]{1,0,2:T(8,128)}) fusion(pred[384,3072]{0,1:T(8,128)(4,1)S(1)} %broadcast_compare_fusion, bf16[3072,128]{1,0:T(8,128)(2,1)S(1)} %all_gather.9, bf16[384,1024]{1,0:T(8,128)(2,1)S(1)} %copy-done), kind=kOutput, calls=%fused_computation.5 | convolution fusion | flops 2444227584 | bytes 40513536 | tf_op jit(solution)/shard_map/qhd,kd->hqk/dot_general | solution.py:23
  41.9 16.3 %all_gather.10 = bf16[3072,128]{0,1:T(8,128)(2,1)S(1)} all-gather(bf16[384,128]{0,1:T(8,128)(2,1)S(1)} %copy.49), channel_id=1, replica_groups=mesh['dp'=2,'ctx'=8,'exp'=8] {'ctx'}, dimensions={0}, use_global_device_ids=true | all-gather | bytes 884736 | tf_op jit(solution)/shard_map/all_gather | solution.py:67
  58.3 16.8 %fusion.1 = f32[8,384]{1,0:T(8,128)S(1)} fusion(f32[3072,384,8]{1,0,2:T(8,128)} %get-tuple-element.8, f32[8,384]{1,0:T(8,128)S(1)} %broadcast_maximum_fusion, pred[384,3072]{0,1:T(8,128)(4,1)S(1)} %broadcast_compare_fusion), kind=kLoop, calls=%fused_computation.6 | loop fusion | flops 47182848 | bytes 38952960 | tf_op jit(solution)/shard_map/reduce_sum | solution.py:29
  75.1 16.3 %fusion.14 = bf16[384,8,128]{0,2,1:T(8,128)(2,1)S(1)} fusion(f32[3072,384,8]{1,0,2:T(8,128)} %get-tuple-element.8, f32[8,384]{1,0:T(8,128)S(1)} %broadcast_maximum_fusion, pred[384,3072]{0,1:T(8,128)(4,1)S(1)} %broadcast_compare_fusion, bf16[3072,128]{0,1:T(8,128)(2,1)S(1)} %all_gather.10, f32[384,8]{0,1:T(8,128)S(1)} %bitcast.75), kind=kOutput, calls=%fused_computation.22 | convolution fusion | flops 2463891456 | bytes 40525824 | tf_op jit(solution)/shard_map/hqk,kd->hqd/dot_general | solution.py:30
  91.4 0.0 all-gather.2.cloned.1.call-done
  91.4 0.0 copy-start.6
  91.4 8.5 %convolution_convert_fusion.1 = bf16[384,4096]{1,0:T(8,128)(2,1)} fusion(bf16[384,1024]{0,1:T(8,128)(2,1)S(1)} %bitcast.77, bf16[1024,4096]{1,0:T(8,128)(2,1)} %all-gather.2.cloned.1.call-done), kind=kOutput, calls=%fused_computation.18 | convolution fusion | flops 3222798336 | bytes 12320768 | tf_op jit(solution)/shard_map/dot_general | solution.py:79
  100.0 0.0 reduce-scatter.2.cloned.1.call-update
  100.0 0.1 copy.42
  100.1 0.1 eq.64
  100.2 0.1 eq.60
  100.3 0.1 reshape.149
  100.4 0.9 reduce-window.6
  101.3 0.2 slice_reduce_fusion
  101.5 0.1 fusion.24
  101.7 20.4 %scatter_fusion = s32[64,12]{0,1:T(8,128)S(1)} fusion(s32[64,12]{0,1:T(8,128)S(1)} %broadcast_in_dim.80, s32[384]{0:T(512)S(1)} %get-tuple-element.6, s32[384]{0:T(512)S(1)} %add_select_fusion.1), kind=kCustom, calls=%fused_computation.2 | custom fusion | bytes 7680 | tf_op jit(solution)/shard_map/scatter | solution.py:106
  122.1 0.1 copy.46
  122.2 0.1 reshape.156
  122.4 58.9 %reduce-scatter.2.cloned.1.call-done = bf16[48,4096]{1,0:T(8,128)(2,1)} async-done(((bf16[384,4096]{1,0:T(8,128)(2,1)}), bf16[48,4096]{1,0:T(8,128)(2,1)}) %reduce-scatter.2.cloned.1.call-update) | async-done | bytes 393232 | tf_op jit(solution)/shard_map/reduce_scatter | solution.py:85
  181.3 0.0 copy-done.3
  181.3 1.3 multiply_reduce_fusion
  182.6 1.2 multiply_convert_fusion.1
  183.8 5.8 %gather_fusion = bf16[768,4096]{1,0:T(8,128)(2,1)} fusion(bf16[49,4096]{1,0:T(8,128)(2,1)S(1)} %concatenate.7, s32[1024]{0:T(1024)S(1)} %pad_clamp_fusion), kind=kCustom, calls=%fused_computation | custom fusion | bytes 12585984 | tf_op jit(solution)/shard_map/gather | solution.py:109
  189.6 9.8 %reshape.155 = bf16[64,12,4096]{2,1,0:T(8,128)(2,1)} reshape(bf16[768,4096]{1,0:T(8,128)(2,1)} %gather_fusion) | data formatting | bytes 12582912 | tf_op jit(solution)/shard_map/gather | solution.py:109
  199.3 106.7 %all_to_all.10 = bf16[64,12,4096]{2,1,0:T(8,128)(2,1)} all-to-all(bf16[64,12,4096]{2,1,0:T(8,128)(2,1)} %reshape.155), channel_id=1, replica_groups=mesh['dp'=2,'ctx'=8,'exp'=8] {'ctx','exp'}, dimensions={0} | all-to-all | bytes 12582912 | tf_op jit(solution)/shard_map/all_to_all | solution.py:110
  306.1 10.0 %reshape.151 = bf16[768,4096]{1,0:T(8,128)(2,1)} reshape(bf16[64,12,4096]{2,1,0:T(8,128)(2,1)} %all_to_all.10) | data formatting | bytes 12582912 | tf_op jit(solution)/shard_map/reshape | solution.py:111
  316.0 9.1 %fusion.10 = f32[768,768]{1,0:T(8,128)S(1)} fusion(bf16[768,4096]{1,0:T(8,128)(2,1)} %reshape.151, bf16[1,4096,768]{2,1,0:T(8,128)(2,1)} %param.21), kind=kOutput, calls=%fused_computation.16 | convolution fusion | flops 4831838208 | bytes 14942208 | tf_op jit(solution)/shard_map/dot_general | solution.py:112
  325.1 8.0 %multiply_convert_fusion = bf16[768,768]{1,0:T(8,128)(2,1)S(1)} fusion(f32[768,768]{1,0:T(8,128)S(1)} %fusion.10, bf16[768,4096]{1,0:T(8,128)(2,1)S(1)} %copy-done.2, bf16[1,4096,768]{2,1,0:T(8,128)(2,1)} %param.22), kind=kOutput, calls=%fused_computation.19 | convolution fusion | flops 4835377152 | bytes 16121856 | tf_op jit(solution)/shard_map/dot_general | solution.py:113
  333.1 9.8 %convolution_convert_fusion = bf16[768,4096]{1,0:T(8,128)(2,1)} fusion(bf16[768,768]{1,0:T(8,128)(2,1)S(1)} %multiply_convert_fusion, bf16[1,768,4096]{2,1,0:T(8,128)(2,1)} %param.23), kind=kOutput, calls=%fused_computation.10 | convolution fusion | flops 4834983936 | bytes 13762560 | tf_op jit(solution)/shard_map/dot_general | solution.py:115
  343.0 9.7 %reshape.152 = bf16[64,12,4096]{2,1,0:T(8,128)(2,1)} reshape(bf16[768,4096]{1,0:T(8,128)(2,1)} %convolution_convert_fusion) | data formatting | bytes 12582912 | tf_op jit(solution)/shard_map/reshape | solution.py:119
  352.7 6.0 %all-to-all-start.1 = ((bf16[64,12,4096]{2,1,0:T(8,128)(2,1)}), bf16[64,12,4096]{2,1,0:T(8,128)(2,1)}, u32[]{:S(2)}, u32[]{:S(2)}) async-start(bf16[64,12,4096]{2,1,0:T(8,128)(2,1)} %reshape.152), calls=%async_computation.2 | async-start | bytes 16777216 | tf_op jit(solution)/shard_map/all_to_all | solution.py:118
  358.7 0.0 copy-done.7
  358.7 0.1 copy.41
  358.8 100.0 %all-to-all-done.1 = bf16[64,12,4096]{2,1,0:T(8,128)(2,1)} async-done(((bf16[64,12,4096]{2,1,0:T(8,128)(2,1)}), bf16[64,12,4096]{2,1,0:T(8,128)(2,1)}, u32[]{:S(2)}, u32[]{:S(2)}) %all-to-all-start.1) | async-done | bytes 6291488 | tf_op jit(solution)/shard_map/all_to_all | solution.py:118
  458.8 9.5 %copy.47 = bf16[64,12,4096]{2,0,1:T(8,128)(2,1)} copy(bf16[64,12,4096]{2,1,0:T(8,128)(2,1)} %all-to-all-done.1) | data formatting | bytes 12582912 | tf_op jit(solution)/shard_map/all_to_all | solution.py:118
  468.3 17.7 %gather_fusion.1 = bf16[384,4096]{1,0:T(8,128)(2,1)} fusion(bf16[64,12,4096]{2,0,1:T(8,128)(2,1)} %copy.47, s32[384]{0:T(512)S(1)} %get-tuple-element.5), kind=kCustom, calls=%fused_computation.1 | custom fusion | bytes 6294528 | tf_op jit(solution)/shard_map/gather | solution.py:121
  486.1 4.5 fusion.6
  490.5 0.9 add_convert_fusion
  (27 shorter events, 0.2 us)
Async XLA Ops:
  6.5 20.8 %copy-start = (bf16[384,1024]{1,0:T(8,128)(2,1)S(1)}, bf16[384,1024]{1,0:T(8,128)(2,1)}, u32[]{:S(2)}) copy-start(bf16[384,1024]{1,0:T(8,128)(2,1)} %param.12) | copy-start | bytes 2359300
  6.5 84.8 %all-gather.2.cloned.1.call-start = ((), (), s32[]{:S(2)}) async-start(), calls=%async_computation.3 | async-start | bytes 9437184 | tf_op jit(solution)/shard_map/all_gather | solution.py:81
  7.3 174.0 %reduce-scatter.2.cloned.1.call-start = ((), (), s32[]{:S(2)}) async-start(), calls=%async_computation.4 | async-start | bytes 3538944 | tf_op jit(solution)/shard_map/reduce_scatter | solution.py:85
  91.4 8.6 %copy-start.6 = (s32[48,8]{0,1:T(8,128)S(1)}, s32[48,8]{0,1:T(8,128)}, u32[]{:S(2)}) copy-start(s32[48,8]{0,1:T(8,128)} %param.19) | copy-start | bytes 4612
  100.0 81.3 %copy-start.3 = (bf16[48,4096]{1,0:T(8,128)(2,1)S(1)}, bf16[48,4096]{1,0:T(8,128)(2,1)}, u32[]{:S(2)}) copy-start(bf16[48,4096]{1,0:T(8,128)(2,1)} %param.17) | copy-start | bytes 1179652
  100.0 82.6 %copy-start.5 = (f32[4096]{0:T(1024)S(1)}, f32[4096]{0:T(1024)}, u32[]{:S(2)}) copy-start(f32[4096]{0:T(1024)} %param.18) | copy-start | bytes 49156
  316.0 9.1 %copy-start.2 = (bf16[768,4096]{1,0:T(8,128)(2,1)S(1)}, bf16[768,4096]{1,0:T(8,128)(2,1)}, u32[]{:S(2)}) copy-start(bf16[768,4096]{1,0:T(8,128)(2,1)} %reshape.151) | copy-start | bytes 18874372
  352.7 6.0 %copy-start.7 = (f32[48,8]{0,1:T(8,128)S(1)}, f32[48,8]{0,1:T(8,128)}, u32[]{:S(2)}) copy-start(f32[48,8]{0,1:T(8,128)} %param.20) | copy-start | bytes 4612
  352.7 106.1 %all-to-all-start.1 = ((bf16[64,12,4096]{2,1,0:T(8,128)(2,1)}), bf16[64,12,4096]{2,1,0:T(8,128)(2,1)}, u32[]{:S(2)}, u32[]{:S(2)}) async-start(bf16[64,12,4096]{2,1,0:T(8,128)(2,1)} %reshape.152), calls=%async_computation.2 | async-start | bytes 16777216 | tf_op jit(solution)/shard_map/all_to_all | solution.py:118
  468.3 22.2 %copy-start.4 = (bf16[48,4096]{1,0:T(8,128)(2,1)S(1)}, bf16[48,4096]{1,0:T(8,128)(2,1)}, u32[]{:S(2)}) copy-start(bf16[48,4096]{1,0:T(8,128)(2,1)} %reduce-scatter.2.cloned.1.call-done) | copy-start | bytes 1179652
  468.3 23.1 %copy-start.1 = (bf16[384,1024]{1,0:T(8,128)(2,1)S(1)}, bf16[384,1024]{1,0:T(8,128)(2,1)}, u32[]{:S(2)}) copy-start(bf16[384,1024]{1,0:T(8,128)(2,1)} %param.12) | copy-start | bytes 2359300
Sparse Core Ops, SparseCore 0:
  9.1 57.4 all-gather.1
  100.1 81.1 reduce-scatter.1
where the time goes:
time: 508 us; the launch traced here: 499 us
  waiting for transfers between devices  160 us (31%)
  blocking collectives  138 us (27%)
  local copies, waits for them, and re-layouts  85.8 us (17%)
  matrix products  66.4 us (13%)
  other arithmetic  28.6 us (6%)
  between operations  13.9 us (3%)
  starting transfers between devices  6.04 us (1%)
    all_to_all x1, blocking collectives, shards(): lax.all_to_all(outgoing, ('ctx', 'exp'), split_axis=0, concat_axis=0, til...  107 us
    all_to_all x1, waiting for transfers between devices, shards(): lax.all_to_all(produced.reshape(arrived.shape), ('ctx', 'exp'), split_axi...  100 us
    reduce_scatter x1, waiting for transfers between devices, shards(): lax.psum_scatter(rounded.astype(jnp.bfloat16), 'exp', scatter_dimension=0...  58.9 us
    scatter x1, local copies, waits for them, and re-layouts, shards(): table = jnp.full((expert_count, capacity), token_rows, jnp.int32).at[flat...  20.4 us
    gather x1, local copies, waits for them, and re-layouts, shards(): picked = returned[flat_ids, ranks].reshape(token_rows, top_count, width)  17.7 us
    reduce_sum x1, other arithmetic, fold_update(): new_sum = jnp.sum(weights, axis=2)  16.8 us
    all_gather x1, blocking collectives, shards(): value_piece = lax.all_gather(value_head, 'ctx', axis=0, tiled=True)  16.3 us
    dot_general x1, matrix products, fold_update(): jnp.einsum('hqk,kd->hqd', weights.astype(jnp.bfloat16), value_piece, pref...  16.3 us
  transfers between devices with their start and end apart: 3, of which 2 were waited for; matrix products, arithmetic and copies ran while one was open for 15% of the time, Pallas kernels for 0%

commit v1 on v0

--- a/solution.py
+++ b/solution.py
@@ -1,14 +1,27 @@
 import jax
 import jax.numpy as jnp
 from jax import lax
+from jax.experimental import pallas as pl
+from jax.experimental.pallas import tpu as pltpu
 from jax.sharding import PartitionSpec as P
 
 HQ = 64
 KVH = 4
 HD = 128
-
+D = 4096
+HALF = D // 2
+FF = 768
+TOK = 48
+CAP = 12
+PEERS = 8
+BLK = PEERS * CAP
+SLOTS = PEERS * BLK
+SPAN = PEERS * TOK
 
 NEG_FILL = -1e30
+MESH = pl.DeviceIdType.MESH
+F32 = jnp.float32
+BF16 = jnp.bfloat16
 
 
 def span_positions(offsets, owners, within):
@@ -33,25 +46,307 @@
     return (new_max, new_sum, mixed)
 
 
+def route_codes(packed, experts):
+    named = packed[None, :8] == experts.astype(F32)[:, None, None]
+    member = jnp.any(named, axis=1)
+    prob = jnp.sum(jnp.where(named, packed[None, 8:], 0.0), axis=1)
+    t = lax.iota(jnp.int32, SPAN)
+    earlier = (t[:, None] < t[None, :]) & (t[:, None] // TOK == t[None, :] // TOK)
+    rank = jnp.dot(member.astype(BF16), earlier.astype(BF16), preferred_element_type=F32)
+    code = jnp.where(member, (t // TOK * CAP)[None, :] + rank.astype(jnp.int32), -1)
+    return code, prob
+
+
+def moe_kernel(
+    hid_ref, nrm_ref, code_a, code_b, prob_a, prob_b, perm_ref, wg_hbm, wu_hbm, wd_hbm,
+    out_ref,
+    gat_a, gat_b, snd_a, snd_b, arr_a, arr_b, ret_a, ret_b, fin_a, fin_b, prt_a, prt_b,
+    xb, act, act_b, pm, wt, wg, wu, wd,
+    w_sem, s_sem, r_sem,
+):
+    dp, c, e = lax.axis_index("dp"), lax.axis_index("ctx"), lax.axis_index("exp")
+    v = lax.rem(dp + e, 2)
+
+    def at_exp(other):
+        return (lax.rem(v + other, 2), c, other)
+
+    def at_ctx(other):
+        return (dp, other, e)
+
+    weights = [
+        pltpu.make_async_copy(src.at[0], dst, w_sem.at[i])
+        for i, (src, dst) in enumerate(((wg_hbm, wg), (wu_hbm, wu), (wd_hbm, wd)))
+    ]
+    for w in weights:
+        w.start()
+
+    def rows(ref, index, size):
+        return ref.at[pl.ds(pl.multiple_of(index * size, 16), size)]
+
+    def push(src, src_at, dst, mine, other, size, stage, dev):
+        pltpu.make_async_remote_copy(
+            src_ref=rows(src, src_at, size),
+            dst_ref=rows(dst, mine, size),
+            send_sem=s_sem.at[stage, other],
+            recv_sem=r_sem.at[stage, mine],
+            device_id=dev,
+            device_id_type=MESH,
+        ).start()
+
+    def waiter(ref, index, size, stage):
+        return pltpu.make_async_remote_copy(
+            src_ref=rows(ref, index, size),
+            dst_ref=rows(ref, index, size),
+            send_sem=s_sem.at[stage, index],
+            recv_sem=r_sem.at[stage, index],
+            device_id=at_ctx(lax.rem(c + 1, PEERS)),
+            device_id_type=MESH,
+        )
+
+    def wait_all(ref, size, stage, me):
+        def body(i, _):
+            waiter(ref, lax.rem(me + i, PEERS), size, stage).wait_recv()
+            return 0
+        lax.fori_loop(1, PEERS, body, 0)
+
+    def sent_all(ref, size, stage, me):
+        def body(i, _):
+            waiter(ref, lax.rem(me + i, PEERS), size, stage).wait_send()
+            return 0
+        lax.fori_loop(1, PEERS, body, 0)
+
+    barrier = pltpu.get_barrier_semaphore()
+
+    def greet(i, _):
+        pl.semaphore_signal(barrier, 1, device_id=at_exp(lax.rem(e + i, PEERS)), device_id_type=MESH)
+        pl.semaphore_signal(barrier, 1, device_id=at_ctx(lax.rem(c + i, PEERS)), device_id_type=MESH)
+        return 0
+
+    lax.fori_loop(1, PEERS, greet, 0)
+    rows(gat_a, e, TOK)[...] = nrm_ref[:, :HALF]
+    rows(gat_b, c, TOK)[...] = nrm_ref[:, HALF:]
+    pl.semaphore_wait(barrier, 2 * (PEERS - 1))
+
+    def spread(i, _):
+        oe, oc = lax.rem(e + i, PEERS), lax.rem(c + i, PEERS)
+        push(gat_a, e, gat_a, e, oe, TOK, 0, at_exp(oe))
+        push(gat_b, c, gat_b, c, oc, TOK, 1, at_ctx(oc))
+        return 0
+
+    lax.fori_loop(1, PEERS, spread, 0)
+    perm = perm_ref[...]
+    for half in range(2):
+        cols = slice(half * 384, half * 384 + 384)
+        at = lax.broadcasted_iota(jnp.int32, (SLOTS, 384), 1) + half * 384
+        pm[:, cols] = jnp.where(perm == at, 1.0, 0.0).astype(BF16)
+    wait_all(gat_a, TOK, 0, e)
+    wait_all(gat_b, TOK, 1, c)
+
+    slot_of = lax.broadcasted_iota(jnp.int32, (BLK, SPAN), 0)
+
+    def pick(code, index):
+        return jnp.where(code[pl.ds(index, 1), :] == slot_of, 1.0, 0.0).astype(BF16)
+
+    def select(code, gat, pair):
+        hot = jnp.concatenate([pick(code, 2 * pair), pick(code, 2 * pair + 1)], axis=0)
+        return jnp.dot(hot, gat[...], preferred_element_type=F32).astype(BF16)
+
+    def route(i, _):
+        pc, pe = lax.rem(c // 2 + i, 4), lax.rem(e // 2 + i, 4)
+        rows(snd_a, pc, 2 * BLK)[...] = select(code_a, gat_a, pc)
+        for k in range(2):
+            push(snd_a, 2 * pc + k, arr_a, c, 2 * pc + k, BLK, 2, at_ctx(2 * pc + k))
+        rows(snd_b, pe, 2 * BLK)[...] = select(code_b, gat_b, pe)
+        for k in range(2):
+            push(snd_b, 2 * pe + k, arr_b, e, 2 * pe + k, BLK, 3, at_exp(2 * pe + k))
+        return 0
+
+    lax.fori_loop(1, 4, route, 0)
+    pc, pe = c // 2, e // 2
+    sc, se = 2 * pc + 1 - lax.rem(c, 2), 2 * pe + 1 - lax.rem(e, 2)
+    rows(snd_a, pc, 2 * BLK)[...] = select(code_a, gat_a, pc)
+    push(snd_a, sc, arr_a, c, sc, BLK, 2, at_ctx(sc))
+    rows(snd_b, pe, 2 * BLK)[...] = select(code_b, gat_b, pe)
+    push(snd_b, se, arr_b, e, se, BLK, 3, at_exp(se))
+    rows(arr_a, c, BLK)[...] = rows(snd_a, c, BLK)[...]
+    rows(arr_b, e, BLK)[...] = rows(snd_b, e, BLK)[...]
+
+    for w in weights:
+        w.wait()
+    wait_all(arr_b, BLK, 3, e)
+
+    def reorder(n, _):
+        cols = pl.ds(pl.multiple_of(n * 512, 512), 512)
+        xb[:, cols] = jnp.dot(pm[...], arr_b[:, cols], preferred_element_type=F32).astype(BF16)
+        return 0
+
+    lax.fori_loop(0, HALF // 512, reorder, 0)
+    wait_all(arr_a, BLK, 2, c)
+
+    def hidden_tile(k, _):
+        n, m = k // 2, lax.rem(k, 2)
+        cols = pl.ds(pl.multiple_of(n * 256, 256), 256)
+        part = pl.ds(pl.multiple_of(m * 384, 128), 384)
+        a, b = arr_a[part, :], xb[part, :]
+        gate = jnp.dot(a, wg[:HALF, cols], preferred_element_type=F32)
+        gate += jnp.dot(b, wg[HALF:, cols], preferred_element_type=F32)
+        up = jnp.dot(a, wu[:HALF, cols], preferred_element_type=F32)
+        up += jnp.dot(b, wu[HALF:, cols], preferred_element_type=F32)
+        act[part, cols] = (gate / (1.0 + jnp.exp(-gate)) * up).astype(BF16)
+        return 0
+
+    lax.fori_loop(0, 6, hidden_tile, 0)
+    act_b[...] = jnp.dot(pm[...], act[...], preferred_element_type=F32).astype(BF16)
+    sent_all(snd_a, BLK, 2, c)
+    sent_all(snd_b, BLK, 3, e)
+
+    def down(src, pair, first, dst):
+        part = pl.ds(pl.multiple_of(pair * 2 * BLK, 64), 2 * BLK)
+        dst[part, :] = jnp.dot(
+            src[part, :], wd[:, first:first + HALF], preferred_element_type=F32
+        ).astype(BF16)
+
+    def give_back(i, _):
+        pc, pe = lax.rem(c // 2 + i, 4), lax.rem(e // 2 + i, 4)
+        down(act, pc, 0, snd_a)
+        for k in range(2):
+            push(snd_a, 2 * pc + k, ret_a, c, 2 * pc + k, BLK, 4, at_ctx(2 * pc + k))
+        down(act_b, pe, HALF, snd_b)
+        for k in range(2):
+            push(snd_b, 2 * pe + k, ret_b, e, 2 * pe + k, BLK, 5, at_exp(2 * pe + k))
+        return 0
+
+    lax.fori_loop(1, 4, give_back, 0)
+    down(act, pc, 0, snd_a)
+    push(snd_a, sc, ret_a, c, sc, BLK, 4, at_ctx(sc))
+    down(act_b, pe, HALF, snd_b)
+    push(snd_b, se, ret_b, e, se, BLK, 5, at_exp(se))
+    rows(ret_a, c, BLK)[...] = rows(snd_a, c, BLK)[...]
+    rows(ret_b, e, BLK)[...] = rows(snd_b, e, BLK)[...]
+
+    def mix(code, prob, ret, prt):
+        def weigh(i, _):
+            at = pl.ds(pl.multiple_of(i * BLK, 16), BLK)
+            wt[at, :] = jnp.where(
+                code[pl.ds(i, 1), :] == slot_of, prob[pl.ds(i, 1), :], 0.0
+            ).astype(BF16)
+            return 0
+
+        lax.fori_loop(0, PEERS, weigh, 0)
+
+        def tile(n, _):
+            cols = pl.ds(pl.multiple_of(n * 512, 512), 512)
+            prt[:, cols] = lax.dot_general(
+                wt[...], ret[:, cols], (((0,), (0,)), ((), ())), preferred_element_type=F32
+            ).astype(BF16)
+            return 0
+
+        lax.fori_loop(0, HALF // 512, tile, 0)
+
+    wait_all(ret_a, BLK, 4, c)
+    mix(code_a, prob_a, ret_a, prt_a)
+
+    def home_a(i, _):
+        oe = lax.rem(e + i, PEERS)
+        push(prt_a, oe, fin_a, e, oe, TOK, 6, at_exp(oe))
+        return 0
+
+    lax.fori_loop(1, PEERS, home_a, 0)
+    rows(fin_a, e, TOK)[...] = rows(prt_a, e, TOK)[...]
+    wait_all(ret_b, BLK, 5, e)
+    mix(code_b, prob_b, ret_b, prt_b)
+
+    def home_b(i, _):
+        oc = lax.rem(c + i, PEERS)
+        push(prt_b, oc, fin_b, c, oc, TOK, 7, at_ctx(oc))
+        return 0
+
+    lax.fori_loop(1, PEERS, home_b, 0)
+    rows(fin_b, c, TOK)[...] = rows(prt_b, c, TOK)[...]
+
+    wait_all(fin_a, TOK, 6, e)
+    total = hid_ref[:, :HALF]
+    for k in range(PEERS):
+        total += fin_a[k * TOK:(k + 1) * TOK, :].astype(F32)
+    out_ref[:, :HALF] = total.astype(BF16)
+    wait_all(fin_b, TOK, 7, c)
+    total = hid_ref[:, HALF:]
+    for k in range(PEERS):
+        total += fin_b[k * TOK:(k + 1) * TOK, :].astype(F32)
+    out_ref[:, HALF:] = total.astype(BF16)
+
+    sent_all(gat_a, TOK, 0, e)
+    sent_all(gat_b, TOK, 1, c)
+    sent_all(snd_a, BLK, 4, c)
+    sent_all(snd_b, BLK, 5, e)
+    sent_all(prt_a, TOK, 6, e)
+    sent_all(prt_b, TOK, 7, c)
+
+
+def moe(hidden, normed, code_a, code_b, prob_a, prob_b, w_gate, w_up, w_down):
+    i = lax.iota(jnp.int32, SLOTS)
+    perm = (i % BLK // CAP * BLK + i // BLK * CAP + i % CAP)[:, None]
+    vm = pl.BlockSpec(memory_space=pltpu.VMEM)
+    hbm = pl.BlockSpec(memory_space=pl.ANY)
+    return pl.pallas_call(
+        moe_kernel,
+        out_shape=jax.ShapeDtypeStruct((TOK, D), BF16),
+        in_specs=[vm] * 7 + [hbm] * 3,
+        out_specs=vm,
+        scratch_shapes=[
+            pltpu.VMEM((SPAN, HALF), BF16),
+            pltpu.VMEM((SPAN, HALF), BF16),
+            pltpu.VMEM((SLOTS, HALF), BF16),
+            pltpu.VMEM((SLOTS, HALF), BF16),
+            pltpu.VMEM((SLOTS, HALF), BF16),
+            pltpu.VMEM((SLOTS, HALF), BF16),
+            pltpu.VMEM((SLOTS, HALF), BF16),
+            pltpu.VMEM((SLOTS, HALF), BF16),
+            pltpu.VMEM((SPAN, HALF), BF16),
+            pltpu.VMEM((SPAN, HALF), BF16),
+            pltpu.VMEM((SPAN, HALF), BF16),
+            pltpu.VMEM((SPAN, HALF), BF16),
+            pltpu.VMEM((SLOTS, HALF), BF16),
+            pltpu.VMEM((SLOTS, FF), BF16),
+            pltpu.VMEM((SLOTS, FF), BF16),
+            pltpu.VMEM((SLOTS, SLOTS), BF16),
+            pltpu.VMEM((SLOTS, SPAN), BF16),
+            pltpu.VMEM((D, FF), BF16),
+            pltpu.VMEM((D, FF), BF16),
+            pltpu.VMEM((FF, D), BF16),
+            pltpu.SemaphoreType.DMA((3,)),
+            pltpu.SemaphoreType.DMA((8, PEERS)),
+            pltpu.SemaphoreType.DMA((8, PEERS)),
+        ],
+        compiler_params=pltpu.CompilerParams(
+            collective_id=1, has_side_effects=True, vmem_limit_bytes=62 * 1024 * 1024
+        ),
+        cost_estimate=pl.CostEstimate(flops=18_000_000_000, bytes_accessed=20_000_000, transcendentals=600_000),
+        name="moe",
+    )(hidden, normed, code_a, code_b, prob_a, prob_b, perm, w_gate, w_up, w_down)
+
+
 def shards(
-    queries,
-    keys,
-    values,
-    offsets,
-    out_proj,
-    residual,
-    norm_gain,
-    expert_ids,
-    gate_probs,
-    w_gate,
-    w_up,
-    w_down,
+    queries, keys, values, offsets, out_proj, residual, norm_gain, expert_ids, gate_probs, w_gate, w_up, w_down,
 ):
     span = queries.shape[0]
     heads_here = queries.shape[1] // HD
     group_size = HQ // KVH
+    dp_place = lax.axis_index("dp")
     ctx_place = lax.axis_index("ctx")
     exp_place = lax.axis_index("exp")
+
+    packed = jnp.concatenate([expert_ids.T.astype(F32), gate_probs.T], axis=0)
+    near = lax.all_gather(packed, ("dp", "exp"), axis=0, tiled=False).reshape(2, PEERS, 16, TOK)
+    which = (dp_place + exp_place + lax.iota(jnp.int32, PEERS)) % 2
+    packed_a = jnp.where(which[:, None, None] == 0, near[0], near[1])
+    packed_b = lax.all_gather(packed, "ctx", axis=0, tiled=False)
+    packed_a = jnp.transpose(packed_a, (1, 0, 2)).reshape(16, SPAN)
+    packed_b = jnp.transpose(packed_b, (1, 0, 2)).reshape(16, SPAN)
+    steps = lax.iota(jnp.int32, PEERS)
+    code_a, prob_a = route_codes(packed_a, steps * PEERS + exp_place)
+    code_b, prob_b = route_codes(packed_b, ctx_place * PEERS + steps)
+
     kv_head = exp_place * heads_here // group_size
     key_head = lax.dynamic_slice_in_dim(keys, kv_head * HD, HD, 1)
     value_head = lax.dynamic_slice_in_dim(values, kv_head * HD, HD, 1)
@@ -88,39 +383,7 @@
     hidden = residual.astype(jnp.float32) + attn_sum
     inverse = lax.rsqrt(jnp.mean(hidden * hidden, axis=1, keepdims=True) + 1e-06)
     normed = (hidden * inverse * norm_gain[None, :]).astype(jnp.bfloat16)
-    token_rows = normed.shape[0]
-    width = normed.shape[1]
-    top_count = expert_ids.shape[1]
-    ctx_count = lax.axis_size("ctx")
-    exp_count = lax.axis_size("exp")
-    expert_count = ctx_count * exp_count
-    capacity = 2 * token_rows * top_count // expert_count
-    flat_ids = expert_ids.reshape(-1)
-    one_hot = (flat_ids[:, None] == lax.iota(jnp.int32, expert_count)[None, :]).astype(jnp.int32)
-    earlier = jnp.cumsum(one_hot, axis=0) - one_hot
-    ranks = jnp.sum(earlier * one_hot, axis=1)
-    owner_rows = lax.iota(jnp.int32, token_rows * top_count) // top_count
-    table = (
-        jnp.full((expert_count, capacity), token_rows, jnp.int32)
-        .at[flat_ids, ranks]
-        .set(owner_rows)
-    )
-    padded = jnp.concatenate([normed, jnp.zeros((1, width), jnp.bfloat16)], axis=0)
-    outgoing = padded[table]
-    arrived = lax.all_to_all(outgoing, ("ctx", "exp"), split_axis=0, concat_axis=0, tiled=True)
-    flat_rows = arrived.reshape(-1, width)
-    gate_proj = jnp.dot(flat_rows, w_gate[0], preferred_element_type=jnp.float32)
-    up_proj = jnp.dot(flat_rows, w_up[0], preferred_element_type=jnp.float32)
-    activated = (jax.nn.silu(gate_proj) * up_proj).astype(jnp.bfloat16)
-    produced = jnp.dot(activated, w_down[0], preferred_element_type=jnp.float32).astype(
-        jnp.bfloat16
-    )
-    returned = lax.all_to_all(
-        produced.reshape(arrived.shape), ("ctx", "exp"), split_axis=0, concat_axis=0, tiled=True
-    )
-    picked = returned[flat_ids, ranks].reshape(token_rows, top_count, width)
-    mixture = jnp.sum(gate_probs[:, :, None] * picked.astype(jnp.float32), axis=1)
-    return (hidden + mixture).astype(jnp.bfloat16)
+    return moe(hidden, normed, code_a, code_b, prob_a, prob_b, w_gate, w_up, w_down)
 
 
 def solution(mesh):

time: 508 us -> 352 us (0.69); the launches traced: 499 us -> 351 us
  Pallas kernels: 0 us -> 156 us
  waiting for transfers between devices: 160 us -> 22.5 us
  local copies, waits for them, and re-layouts: 85.8 us -> 4.09 us
  blocking collectives: 138 us -> 86.7 us
  matrix products: 66.4 us -> 42.4 us
  starting transfers between devices: 6.04 us -> 0.04 us
    pallas_call x0 -> x1, Pallas kernels: none -> 156 us  [moe(): pl.pallas_call(moe_kernel, out_shape=jax.ShapeDtypeStruct((TOK, D), BF16)...]
    all_to_all x1 -> x0, blocking collectives: 107 us -> none  [shards(): lax.all_to_all(outgoing, ('ctx', 'exp'), split_axis=0, concat_axis=0, til...]
    all_to_all x1 -> x0, waiting for transfers between devices: 100 us -> none  [shards(): lax.all_to_all(produced.reshape(arrived.shape), ('ctx', 'exp'), split_axi...]
    all_gather x0 -> x2, blocking collectives: none -> 55.5 us  [the longest x1 35.3 us: shards(): lax.all_gather(packed, ('dp', 'exp'), axis=0, tiled=False)]
    reduce_scatter x1, waiting for transfers between devices: 58.9 us -> 21.8 us  [shards(): lax.psum_scatter(rounded.astype(jnp.bfloat16), 'exp', scatter_dimension=0...]
    gather x3 -> x0, local copies, waits for them, and re-layouts: 33.3 us -> none  [the longest x1 17.7 us: shards(): picked = returned[flat_ids, ranks].reshape(token_rows, top_count, width)]
    dot_general x3 -> x2, matrix products: 26.9 us -> 1.74 us  [route_codes(): jnp.dot(member.astype(BF16), earlier.astype(BF16), preferred_element_type...]
    scatter x1 -> x0, local copies, waits for them, and re-layouts: 20.4 us -> none  [shards(): table = jnp.full((expert_count, capacity), token_rows, jnp.int32).at[flat...]
  transfers between devices with their start and end apart: 3 -> 2, of which waited for: 2 -> 1; matrix products, arithmetic and copies ran while one was open for 15% -> 17% of each run, Pallas kernels for 0% -> 0%
where the time goes in v1:
time: 352 us; the launch traced here: 351 us
  Pallas kernels  156 us (44%)
  blocking collectives  86.7 us (25%)
  matrix products  42.4 us (12%)
  other arithmetic  25.5 us (7%)
  waiting for transfers between devices  22.5 us (6%)
  between operations  13.6 us (4%)
  local copies, waits for them, and re-layouts  4.09 us (1%)
    pallas_call x1, Pallas kernels, moe(): pl.pallas_call(moe_kernel, out_shape=jax.ShapeDtypeStruct((TOK, D), BF16)...  156 us
    all_gather x1, blocking collectives, shards(): lax.all_gather(packed, ('dp', 'exp'), axis=0, tiled=False)  35.3 us
    reduce_scatter x1, waiting for transfers between devices, shards(): lax.psum_scatter(rounded.astype(jnp.bfloat16), 'exp', scatter_dimension=0...  21.8 us
    all_gather x1, blocking collectives, shards(): packed_b = lax.all_gather(packed, 'ctx', axis=0, tiled=False)  20.2 us
    dot_general x1, matrix products, fold_update(): jnp.einsum('hqk,kd->hqd', weights.astype(jnp.bfloat16), value_piece, pref...  17.3 us
    reduce_sum x1, other arithmetic, fold_update(): new_sum = jnp.sum(weights, axis=2)  16.8 us
    all_gather x1, blocking collectives, shards(): value_piece = lax.all_gather(value_head, 'ctx', axis=0, tiled=True)  16.1 us
    all_gather x1, blocking collectives, shards(): key_piece = lax.all_gather(key_head, 'ctx', axis=0, tiled=True)  15.1 us
  transfers between devices with their start and end apart: 2, of which 1 were waited for; matrix products, arithmetic and copies ran while one was open for 17% of the time, Pallas kernels for 0%

profile of v1, /device:TPU:1, one launch (start us, length us, event | category | flops | bytes accessed | tf_op | source)
XLA Modules:
  0.0 351.1 jit_solution(4983147871556594043)
XLA Ops:
  6.5 0.0 copy-start
  6.5 0.0 all-gather.4.cloned.1.call-start
  6.5 0.7 all-gather.4.cloned.1.call-update
  7.3 0.0 reduce-scatter.2.cloned.1.call-start
  7.3 0.9 constant_dynamic-slice_fusion
  8.2 0.1 copy.29
  8.4 0.9 constant_dynamic-slice_fusion.1
  9.3 0.8 select_reduce_fusion
  10.1 0.7 select_reduce_fusion.1
  10.8 15.1 %all_gather.19 = bf16[3072,128]{1,0:T(8,128)(2,1)S(1)} all-gather(bf16[384,128]{1,0:T(8,128)(2,1)S(1)} %constant_dynamic-slice_fusion.1), channel_id=1, replica_groups=mesh['dp'=2,'ctx'=8,'exp'=8] {'ctx'}, dimensions={0}, use_global_device_ids=true | all-gather | bytes 884736 | tf_op jit(solution)/shard_map/all_gather | solution.py:361
  25.9 1.4 broadcast_compare_fusion
  27.3 0.0 copy-done
  27.3 14.6 %fusion = (f32[8,384]{1,0:T(8,128)S(1)}, f32[3072,384,8]{1,0,2:T(8,128)}) fusion(pred[384,3072]{0,1:T(8,128)(4,1)S(1)} %broadcast_compare_fusion, bf16[3072,128]{1,0:T(8,128)(2,1)S(1)} %all_gather.19, bf16[384,1024]{1,0:T(8,128)(2,1)S(1)} %copy-done), kind=kOutput, calls=%fused_computation.2 | convolution fusion | flops 2444227584 | bytes 40513536 | tf_op jit(solution)/shard_map/qhd,kd->hqk/dot_general | solution.py:36
  41.9 16.1 %all_gather.20 = bf16[3072,128]{0,1:T(8,128)(2,1)S(1)} all-gather(bf16[384,128]{0,1:T(8,128)(2,1)S(1)} %copy.29), channel_id=1, replica_groups=mesh['dp'=2,'ctx'=8,'exp'=8] {'ctx'}, dimensions={0}, use_global_device_ids=true | all-gather | bytes 884736 | tf_op jit(solution)/shard_map/all_gather | solution.py:362
  58.0 16.8 %fusion.1 = f32[8,384]{1,0:T(8,128)S(1)} fusion(f32[3072,384,8]{1,0,2:T(8,128)} %get-tuple-element.14, f32[8,384]{1,0:T(8,128)S(1)} %broadcast_maximum_fusion, pred[384,3072]{0,1:T(8,128)(4,1)S(1)} %broadcast_compare_fusion), kind=kLoop, calls=%fused_computation.3 | loop fusion | flops 47182848 | bytes 38952960 | tf_op jit(solution)/shard_map/reduce_sum | solution.py:42
  74.9 0.0 copy-start.4
  74.9 0.0 copy-start.5
  74.9 0.0 copy-start.2
  74.9 0.0 copy-start.3
  74.9 17.3 %fusion.6 = bf16[384,8,128]{0,2,1:T(8,128)(2,1)} fusion(f32[3072,384,8]{1,0,2:T(8,128)} %get-tuple-element.14, f32[8,384]{1,0:T(8,128)S(1)} %broadcast_maximum_fusion, pred[384,3072]{0,1:T(8,128)(4,1)S(1)} %broadcast_compare_fusion, bf16[3072,128]{0,1:T(8,128)(2,1)S(1)} %all_gather.20, f32[384,8]{0,1:T(8,128)S(1)} %bitcast.55), kind=kOutput, calls=%fused_computation.10 | convolution fusion | flops 2463891456 | bytes 40525824 | tf_op jit(solution)/shard_map/hqk,kd->hqd/dot_general | solution.py:43
  92.2 0.0 all-gather.4.cloned.1.call-done
  92.2 8.8 %convolution_convert_fusion = bf16[384,4096]{1,0:T(8,128)(2,1)} fusion(bf16[384,1024]{0,1:T(8,128)(2,1)} %bitcast.57, bf16[1024,4096]{1,0:T(8,128)(2,1)} %all-gather.4.cloned.1.call-done), kind=kOutput, calls=%fused_computation.7 | convolution fusion | flops 3222798336 | bytes 12320768 | tf_op jit(solution)/shard_map/dot_general | solution.py:374
  101.0 0.0 copy-start.1
  101.0 0.0 reduce-scatter.2.cloned.1.call-update
  101.0 0.0 copy-done.4
  101.0 0.0 copy-done.5
  101.1 35.3 %all-gather = f32[256,48]{1,0:T(8,128)S(1)} all-gather(f32[16,48]{1,0:T(8,128)S(1)} %pad_maximum_fusion), channel_id=2, replica_groups=mesh['dp'=2,'ctx'=8,'exp'=8] {'dp','exp'}, dimensions={0}, use_global_device_ids=true | all-gather | bytes 52224 | tf_op jit(solution)/shard_map/all_gather | solution.py:340
  136.4 0.1 fusion.49
  136.5 0.1 eq.105
  136.5 0.1 broadcast_in_dim.122
  136.6 20.2 %all-gather.1 = f32[128,48]{1,0:T(8,128)S(1)} all-gather(f32[16,48]{1,0:T(8,128)S(1)} %pad_maximum_fusion), channel_id=3, replica_groups=mesh['dp'=2,'ctx'=8,'exp'=8] {'ctx'}, dimensions={0}, use_global_device_ids=true | all-gather | bytes 27648 | tf_op jit(solution)/shard_map/all_gather | solution.py:343
  156.9 0.1 eq.112
  157.0 0.1 broadcast_in_dim.125
  157.1 0.1 compare_reduce_fusion.1
  157.2 0.1 compare_reduce_fusion
  157.3 0.7 fusion.47
  158.0 1.3 fusion.33.perm_ref
  159.3 0.9 fusion.12.code_a
  160.2 0.9 fusion.10.code_b
  161.1 21.8 %reduce-scatter.2.cloned.1.call-done = bf16[48,4096]{1,0:T(8,128)(2,1)} async-done(((bf16[384,4096]{1,0:T(8,128)(2,1)}), bf16[48,4096]{1,0:T(8,128)(2,1)}) %reduce-scatter.2.cloned.1.call-update) | async-done | bytes 393232 | tf_op jit(solution)/shard_map/reduce_scatter | solution.py:380
  182.8 0.0 copy-done.2
  182.8 1.2 multiply_reduce_fusion
  184.1 0.0 copy-done.3
  184.1 2.1 multiply_convert_fusion
  186.2 156.3 %moe.1 = bf16[48,4096]{1,0:T(8,128)(2,1)} custom-call(f32[48,4096]{1,0:T(8,128)} %get-tuple-element.6.hid_ref, bf16[48,4096]{1,0:T(8,128)(2,1)} %get-tuple-element.5.nrm_ref, s32[8,384]{1,0:T(8,128)} %fusion.12.code_a, s32[8,384]{1,0:T(8,128)} %fusion.10.code_b, f32[8,384]{1,0:T(8,128)} %get-tuple-element.17.prob_a, f32[8,384]{1,0:T(8,128)} %get-tuple-element.18.prob_b, ...), custom_call_target="tpu_custom_call" | custom-call | flops 17999998976 | bytes 20000000 | tf_op jit(solution)/shard_map/moe/pallas_call | solution.py:291
  342.5 1.8 copy.44
  344.3 0.0 copy-done.1
  (16 shorter events, 0.1 us)
Async XLA Ops:
  6.5 20.8 %copy-start = (bf16[384,1024]{1,0:T(8,128)(2,1)S(1)}, bf16[384,1024]{1,0:T(8,128)(2,1)}, u32[]{:S(2)}) copy-start(bf16[384,1024]{1,0:T(8,128)(2,1)} %param.12) | copy-start | bytes 2359300
  6.5 85.7 %all-gather.4.cloned.1.call-start = ((), (), s32[]{:S(2)}) async-start(), calls=%async_computation.1 | async-start | bytes 9437184 | tf_op jit(solution)/shard_map/all_gather | solution.py:376
  7.3 175.6 %reduce-scatter.2.cloned.1.call-start = ((), (), s32[]{:S(2)}) async-start(), calls=%async_computation.2 | async-start | bytes 3538944 | tf_op jit(solution)/shard_map/reduce_scatter | solution.py:380
  74.9 26.1 %copy-start.4 = (s32[48,8]{0,1:T(8,128)S(1)}, s32[48,8]{0,1:T(8,128)}, u32[]{:S(2)}) copy-start(s32[48,8]{0,1:T(8,128)} %param.19) | copy-start | bytes 4612
  74.9 26.1 %copy-start.5 = (f32[48,8]{0,1:T(8,128)S(1)}, f32[48,8]{0,1:T(8,128)}, u32[]{:S(2)}) copy-start(f32[48,8]{0,1:T(8,128)} %param.20) | copy-start | bytes 4612
  74.9 107.9 %copy-start.2 = (bf16[48,4096]{1,0:T(8,128)(2,1)S(1)}, bf16[48,4096]{1,0:T(8,128)(2,1)}, u32[]{:S(2)}) copy-start(bf16[48,4096]{1,0:T(8,128)(2,1)} %param.17) | copy-start | bytes 1179652
  74.9 109.2 %copy-start.3 = (f32[4096]{0:T(1024)S(1)}, f32[4096]{0:T(1024)}, u32[]{:S(2)}) copy-start(f32[4096]{0:T(1024)} %param.18) | copy-start | bytes 49156
  101.0 243.3 %copy-start.1 = (bf16[384,1024]{1,0:T(8,128)(2,1)S(1)}, bf16[384,1024]{1,0:T(8,128)(2,1)}, u32[]{:S(2)}) copy-start(bf16[384,1024]{1,0:T(8,128)(2,1)} %param.12) | copy-start | bytes 2359300
Sparse Core Ops, SparseCore 0:
  9.1 57.4 all-gather.3
  101.1 81.6 reduce-scatter.1

commit v2 on v1

--- a/solution.py
+++ b/solution.py
@@ -1,3 +1,5 @@
+import math
+
 import jax
 import jax.numpy as jnp
 from jax import lax
@@ -5,7 +7,6 @@
 from jax.experimental.pallas import tpu as pltpu
 from jax.sharding import PartitionSpec as P
 
-HQ = 64
 KVH = 4
 HD = 128
 D = 4096
@@ -17,6 +18,7 @@
 BLK = PEERS * CAP
 SLOTS = PEERS * BLK
 SPAN = PEERS * TOK
+HEADS = 8 * HD
 
 NEG_FILL = -1e30
 MESH = pl.DeviceIdType.MESH
@@ -24,44 +26,31 @@
 BF16 = jnp.bfloat16
 
 
-def span_positions(offsets, owners, within):
-    slot_ids = lax.iota(jnp.int32, offsets.shape[0])
-    table = jnp.where(owners[:, None] == slot_ids[None, :], offsets[None, :], 0)
-    return jnp.sum(table, axis=1) + within
-
-
-def fold_update(carry, key_piece, value_piece, query_block, query_pos, key_pos):
-    run_max, run_sum, run_acc = carry
-    visible = key_pos[None, :] <= query_pos[:, None]
-    scores = jnp.einsum(
-        "qhd,kd->hqk", query_block, key_piece, preferred_element_type=jnp.float32
-    ) * HD ** (-0.5)
-    scores = jnp.where(visible[None], scores, NEG_FILL)
-    new_max = jnp.maximum(run_max, jnp.max(scores, axis=2))
-    weights = jnp.where(visible[None], jnp.exp(scores - new_max[:, :, None]), 0.0)
-    new_sum = jnp.sum(weights, axis=2)
-    mixed = jnp.einsum(
-        "hqk,kd->hqd", weights.astype(jnp.bfloat16), value_piece, preferred_element_type=jnp.float32
-    )
-    return (new_max, new_sum, mixed)
-
-
-def route_codes(packed, experts):
-    named = packed[None, :8] == experts.astype(F32)[:, None, None]
-    member = jnp.any(named, axis=1)
-    prob = jnp.sum(jnp.where(named, packed[None, 8:], 0.0), axis=1)
-    t = lax.iota(jnp.int32, SPAN)
-    earlier = (t[:, None] < t[None, :]) & (t[:, None] // TOK == t[None, :] // TOK)
-    rank = jnp.dot(member.astype(BF16), earlier.astype(BF16), preferred_element_type=F32)
-    code = jnp.where(member, (t // TOK * CAP)[None, :] + rank.astype(jnp.int32), -1)
-    return code, prob
+def route_table(packed, expert_of, code, prob, member):
+    ids, probs = packed[:8], packed[8:]
+    for j in range(PEERS):
+        named = ids == expert_of(j).astype(F32)
+        member[j:j + 1, :] = jnp.sum(jnp.where(named, 1.0, 0.0), axis=0, keepdims=True)
+        prob[j:j + 1, :] = jnp.sum(jnp.where(named, probs, 0.0), axis=0, keepdims=True)
+
+    def block_of(dim):
+        t = lax.broadcasted_iota(jnp.int32, (SPAN, SPAN), dim)
+        return t, ((t.astype(F32) + 0.5) * (1.0 / TOK)).astype(jnp.int32)
+
+    before, before_block = block_of(0)
+    t, block = block_of(1)
+    earlier = jnp.where((before < t) & (before_block == block), 1.0, 0.0).astype(BF16)
+    inside = member[...]
+    rank = jnp.dot(inside.astype(BF16), earlier, preferred_element_type=F32)
+    code[...] = jnp.where(inside > 0.5, block[:8] * CAP + rank.astype(jnp.int32), -1)
 
 
 def moe_kernel(
-    hid_ref, nrm_ref, code_a, code_b, prob_a, prob_b, perm_ref, wg_hbm, wu_hbm, wd_hbm,
+    hid_ref, nrm_ref, own_a, own_b, perm_ref, wg_hbm, wu_hbm, wd_hbm,
     out_ref,
     gat_a, gat_b, snd_a, snd_b, arr_a, arr_b, ret_a, ret_b, fin_a, fin_b, prt_a, prt_b,
     xb, act, act_b, pm, wt, wg, wu, wd,
+    rts_a, rts_b, code_a, code_b, prob_a, prob_b, member,
     w_sem, s_sem, r_sem,
 ):
     dp, c, e = lax.axis_index("dp"), lax.axis_index("ctx"), lax.axis_index("exp")
@@ -125,10 +114,14 @@
     lax.fori_loop(1, PEERS, greet, 0)
     rows(gat_a, e, TOK)[...] = nrm_ref[:, :HALF]
     rows(gat_b, c, TOK)[...] = nrm_ref[:, HALF:]
+    rows(rts_a, e, 16)[...] = own_a[...]
+    rows(rts_b, c, 16)[...] = own_b[...]
     pl.semaphore_wait(barrier, 2 * (PEERS - 1))
 
     def spread(i, _):
         oe, oc = lax.rem(e + i, PEERS), lax.rem(c + i, PEERS)
+        push(rts_a, e, rts_a, e, oe, 16, 8, at_exp(oe))
+        push(rts_b, c, rts_b, c, oc, 16, 9, at_ctx(oc))
         push(gat_a, e, gat_a, e, oe, TOK, 0, at_exp(oe))
         push(gat_b, c, gat_b, c, oc, TOK, 1, at_ctx(oc))
         return 0
@@ -139,6 +132,14 @@
         cols = slice(half * 384, half * 384 + 384)
         at = lax.broadcasted_iota(jnp.int32, (SLOTS, 384), 1) + half * 384
         pm[:, cols] = jnp.where(perm == at, 1.0, 0.0).astype(BF16)
+    wait_all(rts_a, 16, 8, e)
+    wait_all(rts_b, 16, 9, c)
+    packed_a, packed_b = rts_a[:16, :], rts_b[:16, :]
+    for k in range(1, PEERS):
+        packed_a += rts_a[k * 16:k * 16 + 16, :]
+        packed_b += rts_b[k * 16:k * 16 + 16, :]
+    route_table(packed_a, lambda j: j * PEERS + e, code_a, prob_a, member)
+    route_table(packed_b, lambda j: c * PEERS + j, code_b, prob_b, member)
     wait_all(gat_a, TOK, 0, e)
     wait_all(gat_b, TOK, 1, c)
 
@@ -281,9 +282,11 @@
     sent_all(snd_b, BLK, 5, e)
     sent_all(prt_a, TOK, 6, e)
     sent_all(prt_b, TOK, 7, c)
-
-
-def moe(hidden, normed, code_a, code_b, prob_a, prob_b, w_gate, w_up, w_down):
+    sent_all(rts_a, 16, 8, e)
+    sent_all(rts_b, 16, 9, c)
+
+
+def moe(hidden, normed, own_a, own_b, w_gate, w_up, w_down):
     i = lax.iota(jnp.int32, SLOTS)
     perm = (i % BLK // CAP * BLK + i // BLK * CAP + i % CAP)[:, None]
     vm = pl.BlockSpec(memory_space=pltpu.VMEM)
@@ -291,7 +294,7 @@
     return pl.pallas_call(
         moe_kernel,
         out_shape=jax.ShapeDtypeStruct((TOK, D), BF16),
-        in_specs=[vm] * 7 + [hbm] * 3,
+        in_specs=[vm] * 5 + [hbm] * 3,
         out_specs=vm,
         scratch_shapes=[
             pltpu.VMEM((SPAN, HALF), BF16),
@@ -314,76 +317,289 @@
             pltpu.VMEM((D, FF), BF16),
             pltpu.VMEM((D, FF), BF16),
             pltpu.VMEM((FF, D), BF16),
+            pltpu.VMEM((PEERS * 16, SPAN), F32),
+            pltpu.VMEM((PEERS * 16, SPAN), F32),
+            pltpu.VMEM((PEERS, SPAN), jnp.int32),
+            pltpu.VMEM((PEERS, SPAN), jnp.int32),
+            pltpu.VMEM((PEERS, SPAN), F32),
+            pltpu.VMEM((PEERS, SPAN), F32),
+            pltpu.VMEM((PEERS, SPAN), F32),
             pltpu.SemaphoreType.DMA((3,)),
-            pltpu.SemaphoreType.DMA((8, PEERS)),
-            pltpu.SemaphoreType.DMA((8, PEERS)),
+            pltpu.SemaphoreType.DMA((10, PEERS)),
+            pltpu.SemaphoreType.DMA((10, PEERS)),
         ],
         compiler_params=pltpu.CompilerParams(
             collective_id=1, has_side_effects=True, vmem_limit_bytes=62 * 1024 * 1024
         ),
         cost_estimate=pl.CostEstimate(flops=18_000_000_000, bytes_accessed=20_000_000, transcendentals=600_000),
         name="moe",
-    )(hidden, normed, code_a, code_b, prob_a, prob_b, perm, w_gate, w_up, w_down)
+    )(hidden, normed, own_a, own_b, perm, w_gate, w_up, w_down)
+
+
+def attn_kernel(
+    off_ref, q_ref, k_hbm, v_hbm, w_hbm, res_ref, gain_ref,
+    hid_ref, nrm_ref,
+    kv, wbuf, mx, acc, att, pbuf, rbuf, tot, zsnd, zbuf,
+    l_sem, kv_s, kv_r, w_s, w_r, y_s, y_r, z_s, z_r,
+):
+    dp, c, e = lax.axis_index("dp"), lax.axis_index("ctx"), lax.axis_index("exp")
+    x, core, y, zh = c // 2, lax.rem(c, 2), e // 2, lax.rem(e, 2)
+    sib = 2 * x + 1 - core
+
+    def at_x(i):
+        return (dp, 2 * lax.rem(x + i, 4) + core, e)
+
+    def at_y(i):
+        return (dp, c, 2 * lax.rem(y + i, 4) + zh)
+
+    at_sib = (dp, sib, e)
+    at_z = (dp, c, 2 * y + 1 - zh)
+
+    def rows(ref, index, size):
+        return ref.at[pl.ds(pl.multiple_of(index * size, 16), size)]
+
+    def remote(src, dst, s, r, dev):
+        return pltpu.make_async_remote_copy(
+            src_ref=src, dst_ref=dst, send_sem=s, recv_sem=r, device_id=dev, device_id_type=MESH
+        )
+
+    kv_head = lax.rem(y, KVH)
+    cols = pl.ds(pl.multiple_of(kv_head * HD, HD), HD)
+    own = rows(kv, c, SPAN)
+    loads = [
+        pltpu.make_async_copy(k_hbm.at[:, cols], own.at[:, :HD], l_sem.at[0]),
+        pltpu.make_async_copy(v_hbm.at[:, cols], own.at[:, HD:], l_sem.at[1]),
+        pltpu.make_async_copy(w_hbm, rows(wbuf, c, HEADS), l_sem.at[2]),
+    ]
+    for load in loads:
+        load.start()
+    barrier = pltpu.get_barrier_semaphore()
+    peers = [at_x(i) for i in (1, 2, 3)] + [at_y(i) for i in (1, 2, 3)] + [at_sib, at_z]
+    for dev in peers:
+        pl.semaphore_signal(barrier, 1, device_id=dev, device_id_type=MESH)
+    loads[0].wait()
+    loads[1].wait()
+    pl.semaphore_wait(barrier, len(peers))
+
+    def copies(buf, size, s, r):
+        def direct(i):
+            return remote(rows(buf, c, size), rows(buf, c, size), s.at[i], r.at[i], at_x(i))
+
+        def arrival(i):
+            block = rows(buf, 2 * lax.rem(x + 4 - i, 4) + core, size)
+            return remote(block, block, s.at[3 + i], r.at[i], at_sib)
+
+        def handed(i):
+            block = rows(buf, 2 * lax.rem(x + 4 - i, 4) + core, size)
+            return remote(block, block, s.at[3 + i], r.at[3 + i], at_sib)
+
+        def handed_arrival(i):
+            block = rows(buf, 2 * lax.rem(x + 4 - i, 4) + 1 - core, size)
+            return remote(block, block, s.at[3 + i], r.at[3 + i], at_sib)
+
+        to_sib = remote(rows(buf, c, size), rows(buf, c, size), s.at[0], r.at[0], at_sib)
+        from_sib = remote(rows(buf, sib, size), rows(buf, sib, size), s.at[0], r.at[0], at_sib)
+        return direct, arrival, handed, handed_arrival, to_sib, from_sib
+
+    k_direct, k_arrival, k_handed, k_handed_arrival, k_to_sib, k_from_sib = copies(kv, SPAN, kv_s, kv_r)
+    w_direct, w_arrival, w_handed, w_handed_arrival, w_to_sib, w_from_sib = copies(wbuf, HEADS, w_s, w_r)
+    k_to_sib.start()
+    for i in (1, 3, 2):
+        k_direct(i).start()
+
+    scale = HD ** (-0.5) * math.log2(math.e)
+    lane = lax.broadcasted_iota(jnp.int32, (1, 2 * SPAN), 1)
+    ones = jnp.ones((2 * SPAN, HD), BF16)
+
+    def group(i):
+        chip = lax.rem(x + 4 - i, 4)
+        at = pl.ds(pl.multiple_of(chip * 2 * SPAN, 2 * SPAN), 2 * SPAN)
+        first, second = off_ref[2 * chip], off_ref[2 * chip + 1]
+        key_pos = jnp.where(lane < SPAN, first + lane, second + lane - SPAN)
+        if i:
+            bias = jnp.where(key_pos <= off_ref[c] + SPAN - 1, 0.0, NEG_FILL)
+
+        def head(h, _):
+            hcols = pl.ds(pl.multiple_of(h * HD, HD), HD)
+            mine = pl.ds(pl.multiple_of(h * SPAN, SPAN), SPAN)
+            s = lax.dot_general(
+                q_ref[:, hcols], kv[at, :HD], (((1,), (1,)), ((), ())), preferred_element_type=F32
+            ) * scale
+            if i:
+                s = s + bias
+            else:
+                query_pos = off_ref[c] + lax.broadcasted_iota(jnp.int32, (SPAN, 1), 0)
+                s = jnp.where(key_pos <= query_pos, s, NEG_FILL)
+            top = jnp.max(s, axis=1, keepdims=True)
+            if i:
+                old = mx[mine, :]
+                new = jnp.maximum(old, top)
+                p = jnp.exp2(s - jnp.concatenate([new] * 6, axis=1)).astype(BF16)
+            else:
+                new = jnp.broadcast_to(top, (SPAN, HD))
+                p = jnp.exp2(s - top).astype(BF16)
+            mixed = jnp.dot(
+                p, jnp.concatenate([kv[at, HD:], ones], axis=1), preferred_element_type=F32
+            )
+            if i:
+                keep = jnp.exp2(old - new)
+                mixed = acc[mine, :] * jnp.concatenate([keep, keep], axis=1) + mixed
+            mx[mine, :] = new
+            acc[mine, :] = mixed
+            return 0
+
+        lax.fori_loop(0, 8, head, 0)
+
+    k_from_sib.wait_recv()
+    group(0)
+    loads[2].wait()
+    w_to_sib.start()
+    for i in (1, 3, 2):
+        w_direct(i).start()
+    for i in (1, 3):
+        k_arrival(i).wait_recv()
+        k_handed(i).start()
+    k_handed_arrival(1).wait_recv()
+    group(1)
+    k_arrival(2).wait_recv()
+    k_handed(2).start()
+    k_handed_arrival(3).wait_recv()
+    group(3)
+    k_handed_arrival(2).wait_recv()
+    group(2)
+
+    def divide(h, _):
+        hcols = pl.ds(pl.multiple_of(h * HD, HD), HD)
+        mine = pl.ds(pl.multiple_of(h * SPAN, SPAN), SPAN)
+        att[:, hcols] = (acc[mine, :HD] / acc[mine, HD:]).astype(BF16)
+        return 0
+
+    lax.fori_loop(0, 8, divide, 0)
+
+    def piece(k):
+        k2 = k // 2
+        chip = lax.rem(x + 4 - lax.rem(k2 * (k2 + 1) // 2, 4), 4)
+        return 2 * chip + lax.rem(core + k, 2)
+
+    def to_y(w, i):
+        return remote(
+            rows(pbuf, w * 4 + lax.rem(y + i, 4), 2 * TOK), rows(rbuf, w * 3 + i - 1, 2 * TOK),
+            y_s.at[w, i - 1], y_r.at[w, i - 1], at_y(i),
+        )
+
+    def to_z(w):
+        return remote(rows(zsnd, w, TOK), rows(zbuf, w, TOK), z_s.at[w], z_r.at[w], at_z)
+
+    def project(k, _):
+        w = piece(k)
+        rows(pbuf, w, SPAN)[...] = jnp.dot(
+            att[...], rows(wbuf, w, HEADS)[...], preferred_element_type=F32
+        ).astype(BF16)
+        for i in (1, 3, 2):
+            to_y(w, i).start()
+        return 0
+
+    def reduce(k, _):
+        w = piece(k)
+        total = rows(pbuf, w * 4 + y, 2 * TOK)[...].astype(F32)
+        for i in (1, 3, 2):
+            to_y(w, i).wait_recv()
+            total += rows(rbuf, w * 3 + i - 1, 2 * TOK)[...].astype(F32)
+        tot[...] = total
+        rows(zsnd, w, TOK)[...] = rows(tot, 1 - zh, TOK)[...].astype(BF16)
+        to_z(w).start()
+        wcols = pl.ds(pl.multiple_of(w * 512, 512), 512)
+        hid_ref[:, wcols] = rows(tot, zh, TOK)[...] + res_ref[:, wcols].astype(F32)
+        return 0
+
+    w_from_sib.wait_recv()
+    lax.fori_loop(0, 2, project, 0)
+    for i in (1, 3):
+        w_arrival(i).wait_recv()
+        w_handed(i).start()
+    for i in (1, 3):
+        w_handed_arrival(i).wait_recv()
+    lax.fori_loop(2, 6, project, 0)
+    w_arrival(2).wait_recv()
+    w_handed(2).start()
+    lax.fori_loop(0, 2, reduce, 0)
+    w_handed_arrival(2).wait_recv()
+    lax.fori_loop(6, 8, project, 0)
+    lax.fori_loop(2, 8, reduce, 0)
+
+    square = jnp.zeros((TOK, 1), F32)
+
+    def finish(k, square):
+        w = piece(k)
+        to_z(w).wait_recv()
+        wcols = pl.ds(pl.multiple_of(w * 512, 512), 512)
+        h = hid_ref[:, wcols] + rows(zbuf, w, TOK)[...].astype(F32)
+        hid_ref[:, wcols] = h
+        return square + jnp.sum(h * h, axis=1, keepdims=True)
+
+    square = lax.fori_loop(0, 8, finish, square)
+    inverse = lax.rsqrt(square * (1.0 / D) + 1e-06)
+    nrm_ref[...] = (hid_ref[...] * inverse * gain_ref[...]).astype(BF16)
+
+    k_to_sib.wait_send()
+    w_to_sib.wait_send()
+    for i in (1, 2, 3):
+        k_direct(i).wait_send()
+        k_handed(i).wait_send()
+        w_direct(i).wait_send()
+        w_handed(i).wait_send()
+
+    def sent(k, _):
+        w = piece(k)
+        for i in (1, 2, 3):
+            to_y(w, i).wait_send()
+        to_z(w).wait_send()
+        return 0
+
+    lax.fori_loop(0, 8, sent, 0)
+
+
+def attend(offsets, queries, keys, values, out_proj, residual, gain):
+    vm = pl.BlockSpec(memory_space=pltpu.VMEM)
+    hbm = pl.BlockSpec(memory_space=pl.ANY)
+    dma = pltpu.SemaphoreType.DMA
+    return pl.pallas_call(
+        attn_kernel,
+        out_shape=(jax.ShapeDtypeStruct((TOK, D), F32), jax.ShapeDtypeStruct((TOK, D), BF16)),
+        in_specs=[pl.BlockSpec(memory_space=pltpu.SMEM), vm, hbm, hbm, hbm, vm, vm],
+        out_specs=(vm, vm),
+        scratch_shapes=[
+            pltpu.VMEM((PEERS * SPAN, 2 * HD), BF16),
+            pltpu.VMEM((PEERS * HEADS, 512), BF16),
+            pltpu.VMEM((8 * SPAN, HD), F32),
+            pltpu.VMEM((8 * SPAN, 2 * HD), F32),
+            pltpu.VMEM((SPAN, HEADS), BF16),
+            pltpu.VMEM((PEERS * SPAN, 512), BF16),
+            pltpu.VMEM((PEERS * 3 * 2 * TOK, 512), BF16),
+            pltpu.VMEM((2 * TOK, 512), F32),
+            pltpu.VMEM((PEERS * TOK, 512), BF16),
+            pltpu.VMEM((PEERS * TOK, 512), BF16),
+            dma((3,)), dma((7,)), dma((7,)), dma((7,)), dma((7,)),
+            dma((PEERS, 3)), dma((PEERS, 3)), dma((PEERS,)), dma((PEERS,)),
+        ],
+        compiler_params=pltpu.CompilerParams(
+            collective_id=2, has_side_effects=True, vmem_limit_bytes=48 * 1024 * 1024
+        ),
+        cost_estimate=pl.CostEstimate(flops=9_000_000_000, bytes_accessed=4_000_000, transcendentals=10_000_000),
+        name="attend",
+    )(offsets, queries, keys, values, out_proj, residual, gain)
 
 
 def shards(
     queries, keys, values, offsets, out_proj, residual, norm_gain, expert_ids, gate_probs, w_gate, w_up, w_down,
 ):
-    span = queries.shape[0]
-    heads_here = queries.shape[1] // HD
-    group_size = HQ // KVH
-    dp_place = lax.axis_index("dp")
-    ctx_place = lax.axis_index("ctx")
-    exp_place = lax.axis_index("exp")
-
     packed = jnp.concatenate([expert_ids.T.astype(F32), gate_probs.T], axis=0)
-    near = lax.all_gather(packed, ("dp", "exp"), axis=0, tiled=False).reshape(2, PEERS, 16, TOK)
-    which = (dp_place + exp_place + lax.iota(jnp.int32, PEERS)) % 2
-    packed_a = jnp.where(which[:, None, None] == 0, near[0], near[1])
-    packed_b = lax.all_gather(packed, "ctx", axis=0, tiled=False)
-    packed_a = jnp.transpose(packed_a, (1, 0, 2)).reshape(16, SPAN)
-    packed_b = jnp.transpose(packed_b, (1, 0, 2)).reshape(16, SPAN)
-    steps = lax.iota(jnp.int32, PEERS)
-    code_a, prob_a = route_codes(packed_a, steps * PEERS + exp_place)
-    code_b, prob_b = route_codes(packed_b, ctx_place * PEERS + steps)
-
-    kv_head = exp_place * heads_here // group_size
-    key_head = lax.dynamic_slice_in_dim(keys, kv_head * HD, HD, 1)
-    value_head = lax.dynamic_slice_in_dim(values, kv_head * HD, HD, 1)
-    own_index = lax.iota(jnp.int32, span)
-    query_pos = span_positions(offsets, jnp.zeros((span,), jnp.int32) + ctx_place, own_index)
-    query_block = queries.reshape(span, heads_here, HD)
-    start_state = (
-        jnp.full((heads_here, span), NEG_FILL, jnp.float32),
-        jnp.zeros((heads_here, span), jnp.float32),
-        jnp.zeros((heads_here, span, HD), jnp.float32),
-    )
-    key_piece = lax.all_gather(key_head, "ctx", axis=0, tiled=True)
-    value_piece = lax.all_gather(value_head, "ctx", axis=0, tiled=True)
-    count = key_piece.shape[0]
-    key_index = lax.iota(jnp.int32, count)
-    key_pos = span_positions(offsets, key_index // span, key_index % span)
-    final_max, final_sum, final_acc = fold_update(
-        start_state, key_piece, value_piece, query_block, query_pos, key_pos
-    )
-    attention = (
-        jnp.transpose(final_acc / final_sum[:, :, None], (1, 0, 2))
-        .reshape(span, heads_here * HD)
-        .astype(jnp.bfloat16)
-    )
-    partial_sum = jnp.dot(
-        attention,
-        lax.all_gather(out_proj, "ctx", axis=1, tiled=True),
-        preferred_element_type=jnp.float32,
-    )
-    rounded = lax.optimization_barrier(partial_sum.astype(jnp.bfloat16)).astype(jnp.float32)
-    attn_sum = lax.psum_scatter(
-        rounded.astype(jnp.bfloat16), "exp", scatter_dimension=0, tiled=True
-    ).astype(jnp.float32)
-    hidden = residual.astype(jnp.float32) + attn_sum
-    inverse = lax.rsqrt(jnp.mean(hidden * hidden, axis=1, keepdims=True) + 1e-06)
-    normed = (hidden * inverse * norm_gain[None, :]).astype(jnp.bfloat16)
-    return moe(hidden, normed, code_a, code_b, prob_a, prob_b, w_gate, w_up, w_down)
+    tiled = jnp.tile(packed, (1, PEERS))
+    block = lax.iota(jnp.int32, SPAN) // TOK
+    own_a = jnp.where(block == lax.axis_index("exp"), tiled, 0.0)
+    own_b = jnp.where(block == lax.axis_index("ctx"), tiled, 0.0)
+    hidden, normed = attend(offsets, queries, keys, values, out_proj, residual, norm_gain[None, :])
+    return moe(hidden, normed, own_a, own_b, w_gate, w_up, w_down)
 
 
 def solution(mesh):

time: 352 us -> 253 us (0.72)
  blocking collectives: 86.7 us -> 0 us
  Pallas kernels: 156 us -> 236 us
  matrix products: 42.4 us -> 0 us
  waiting for transfers between devices: 22.5 us -> 0 us
  other arithmetic: 25.5 us -> 3.32 us
  between operations: 13.6 us -> 0.04 us
  local copies, waits for them, and re-layouts: 4.09 us -> 10.2 us
    all_gather x4 -> x0, blocking collectives: 86.7 us -> none  [the longest x1 35.3 us: shards(): lax.all_gather(packed, ('dp', 'exp'), axis=0, tiled=False)]
    pallas_call x0 -> x1, Pallas kernels: none -> 82 us  [attend(): pl.pallas_call(attn_kernel, out_shape=(jax.ShapeDtypeStruct((TOK, D), F32...]
    dot_general x5 -> x0, matrix products: 42.4 us -> none  [the longest x1 17.3 us: fold_update(): jnp.einsum('hqk,kd->hqd', weights.astype(jnp.bfloat16), value_piece, pref...]
    reduce_scatter x1 -> x0, waiting for transfers between devices: 21.8 us -> none  [shards(): lax.psum_scatter(rounded.astype(jnp.bfloat16), 'exp', scatter_dimension=0...]
    reduce_sum x5 -> x0, other arithmetic: 20.3 us -> none  [the longest x1 16.8 us: fold_update(): new_sum = jnp.sum(weights, axis=2)]
    unnamed x14 -> x19, local copies, waits for them, and re-layouts: 1.92 us -> 10.1 us
  transfers between devices with their start and end apart: 2 -> 0, of which waited for: 1 -> 0; matrix products, arithmetic and copies ran while one was open for 17% -> 0% of each run, Pallas kernels for 0% -> 0%
where the time goes in v2:
time: 253 us; the launch traced here: 249 us
  Pallas kernels  236 us (93%)
  local copies, waits for them, and re-layouts  10.2 us (4%)
  other arithmetic  3.32 us (1%)
    pallas_call x1, Pallas kernels, moe(): pl.pallas_call(moe_kernel, out_shape=jax.ShapeDtypeStruct((TOK, D), BF16)...  153 us
    pallas_call x1, Pallas kernels, attend(): pl.pallas_call(attn_kernel, out_shape=(jax.ShapeDtypeStruct((TOK, D), F32...  82 us
    unnamed x19, local copies, waits for them, and re-layouts  10.1 us

profile of v2, /device:TPU:1, one launch (start us, length us, event | category | flops | bytes accessed | tf_op | source)
XLA Modules:
  0.0 249.1 jit_solution(13099296796751006840)
XLA Ops:
  0.0 0.7 convert_bitcast_fusion
  0.7 0.7 pad_maximum_fusion
  1.4 0.1 tile.10
  1.5 0.6 broadcast_select_fusion
  2.1 1.3 fusion.12.perm_ref
  3.4 0.0 copy-start
  3.4 1.2 copy-done
  4.6 0.0 copy-start.1
  4.6 1.1 copy-done.1
  5.8 0.0 copy-start.2
  5.8 1.0 copy-done.2
  6.8 0.0 copy-start.3
  6.8 1.0 copy-done.3
  7.8 0.0 copy-start.4
  7.8 1.0 copy-done.4
  8.8 0.0 copy-start.5
  8.8 0.7 copy-done.5
  9.5 0.0 copy-start.6
  9.5 0.7 copy-done.6
  10.1 82.0 %attend.1 = (f32[48,4096]{1,0:T(8,128)S(1)}, bf16[48,4096]{1,0:T(8,128)(2,1)S(1)}) custom-call(s32[8]{0:T(128)S(1)} %copy-done.6, bf16[384,1024]{1,0:T(8,128)(2,1)S(1)} %copy-done.1, bf16[384,512]{1,0:T(8,128)(2,1)S(1)} %copy-done.2, bf16[384,512]{1,0:T(8,128)(2,1)S(1)} %copy-done.3, bf16[1024,512]{1,0:T(8,128)(2,1)S(1)} %copy-done, ...), custom_call_target="tpu_custom_call" | custom-call | flops 8999999488 | bytes 4000000 | tf_op jit(solution)/shard_map/attend/pallas_call | solution.py:566
  92.2 0.0 copy-start.7
  92.2 0.9 copy-done.7
  93.1 0.0 copy-start.8
  93.1 0.7 copy-done.8
  93.8 153.5 %moe.1 = bf16[48,4096]{1,0:T(8,128)(2,1)} custom-call(f32[48,4096]{1,0:T(8,128)} %copy-done.7, bf16[48,4096]{1,0:T(8,128)(2,1)} %copy-done.8, f32[16,384]{1,0:T(8,128)} %get-tuple-element.10.own_a, f32[16,384]{1,0:T(8,128)} %get-tuple-element.9.own_b, s32[768,1]{1,0:T(8,128)} %fusion.12.perm_ref, bf16[1,4096,768]{2,1,0:T(8,128)(2,1)} %wg_hbm.1, ...), custom_call_target="tpu_custom_call" | custom-call | flops 17999998976 | bytes 20000000 | tf_op jit(solution)/shard_map/moe/pallas_call | solution.py:294
  247.3 1.8 copy.14
  (2 shorter events, 0.0 us)
Async XLA Ops:
  3.4 1.2 copy-start
  4.6 1.1 copy-start.1
  5.8 1.0 copy-start.2
  6.8 1.0 copy-start.3
  7.8 1.0 copy-start.4
  8.8 0.7 copy-start.5
  9.5 0.7 copy-start.6
  92.2 0.9 copy-start.7
  93.1 0.7 copy-start.8

commit v3 on v2

--- a/solution.py
+++ b/solution.py
@@ -26,16 +26,19 @@
 BF16 = jnp.bfloat16
 
 
-def route_table(packed, expert_of, code, prob, member):
+def route_table(packed, expert_of, first, count, code, prob, member):
     ids, probs = packed[:8], packed[8:]
-    for j in range(PEERS):
+    for j in range(count):
         named = ids == expert_of(j).astype(F32)
-        member[j:j + 1, :] = jnp.sum(jnp.where(named, 1.0, 0.0), axis=0, keepdims=True)
-        prob[j:j + 1, :] = jnp.sum(jnp.where(named, probs, 0.0), axis=0, keepdims=True)
-
+        at = slice(first + j, first + j + 1)
+        member[at, :] = jnp.sum(jnp.where(named, 1.0, 0.0), axis=0, keepdims=True)
+        prob[at, :] = jnp.sum(jnp.where(named, probs, 0.0), axis=0, keepdims=True)
+
+
+def rank_table(code, member):
     def block_of(dim):
         t = lax.broadcasted_iota(jnp.int32, (SPAN, SPAN), dim)
-        return t, ((t.astype(F32) + 0.5) * (1.0 / TOK)).astype(jnp.int32)
+        return t, over(t, TOK)
 
     before, before_block = block_of(0)
     t, block = block_of(1)
@@ -45,22 +48,46 @@
     code[...] = jnp.where(inside > 0.5, block[:8] * CAP + rank.astype(jnp.int32), -1)
 
 
+def over(a, n):
+    return ((a.astype(F32) + 0.5) * (1.0 / n)).astype(jnp.int32)
+
+
 def moe_kernel(
-    hid_ref, nrm_ref, own_a, own_b, perm_ref, wg_hbm, wu_hbm, wd_hbm,
+    hid_ref, nrm_ref, ids_ref, probs_ref, wg_hbm, wu_hbm, wd_hbm,
     out_ref,
-    gat_a, gat_b, snd_a, snd_b, arr_a, arr_b, ret_a, ret_b, fin_a, fin_b, prt_a, prt_b,
+    gat_a, gat_b, snd_a, snd_b, arr_a, arr_b, ret_a, ret_b, fin_a, fin_b, sib_b, zed, zin, tot, keep,
     xb, act, act_b, pm, wt, wg, wu, wd,
     rts_a, rts_b, code_a, code_b, prob_a, prob_b, member,
     w_sem, s_sem, r_sem,
 ):
     dp, c, e = lax.axis_index("dp"), lax.axis_index("ctx"), lax.axis_index("exp")
+    x, core, y, zh = c // 2, lax.rem(c, 2), e // 2, lax.rem(e, 2)
     v = lax.rem(dp + e, 2)
+    sib = 2 * x + 1 - core
 
     def at_exp(other):
         return (lax.rem(v + other, 2), c, other)
 
     def at_ctx(other):
         return (dp, other, e)
+
+    def at_far(other):
+        return (1 - dp, other, 2 * y + 1 - zh)
+
+    def chip_x(i):
+        return lax.rem(x + i, 4)
+
+    def at_x(i):
+        return (dp, 2 * chip_x(i) + core, e)
+
+    def row_y(i):
+        return lax.rem(y + i, 4)
+
+    def at_y(i):
+        return (dp, c, 2 * row_y(i) + zh)
+
+    at_sib = (dp, sib, e)
+    at_z = at_far(c)
 
     weights = [
         pltpu.make_async_copy(src.at[0], dst, w_sem.at[i])
@@ -72,109 +99,164 @@
     def rows(ref, index, size):
         return ref.at[pl.ds(pl.multiple_of(index * size, 16), size)]
 
-    def push(src, src_at, dst, mine, other, size, stage, dev):
-        pltpu.make_async_remote_copy(
-            src_ref=rows(src, src_at, size),
-            dst_ref=rows(dst, mine, size),
-            send_sem=s_sem.at[stage, other],
-            recv_sem=r_sem.at[stage, mine],
-            device_id=dev,
-            device_id_type=MESH,
-        ).start()
-
-    def waiter(ref, index, size, stage):
+    def copy(src, dst, stage, sent, got, dev):
         return pltpu.make_async_remote_copy(
-            src_ref=rows(ref, index, size),
-            dst_ref=rows(ref, index, size),
-            send_sem=s_sem.at[stage, index],
-            recv_sem=r_sem.at[stage, index],
-            device_id=at_ctx(lax.rem(c + 1, PEERS)),
-            device_id_type=MESH,
+            src_ref=src, dst_ref=dst, send_sem=s_sem.at[stage, sent], recv_sem=r_sem.at[stage, got],
+            device_id=dev, device_id_type=MESH,
         )
 
-    def wait_all(ref, size, stage, me):
-        def body(i, _):
-            waiter(ref, lax.rem(me + i, PEERS), size, stage).wait_recv()
-            return 0
-        lax.fori_loop(1, PEERS, body, 0)
-
-    def sent_all(ref, size, stage, me):
-        def body(i, _):
-            waiter(ref, lax.rem(me + i, PEERS), size, stage).wait_send()
-            return 0
-        lax.fori_loop(1, PEERS, body, 0)
+    def same(ref, stage, index):
+        return copy(ref, ref, stage, index, index, at_sib)
 
     barrier = pltpu.get_barrier_semaphore()
 
     def greet(i, _):
-        pl.semaphore_signal(barrier, 1, device_id=at_exp(lax.rem(e + i, PEERS)), device_id_type=MESH)
-        pl.semaphore_signal(barrier, 1, device_id=at_ctx(lax.rem(c + i, PEERS)), device_id_type=MESH)
+        oe, oc = lax.rem(e + i, PEERS), lax.rem(c + i, PEERS)
+        for dev in (at_exp(oe), at_ctx(oc), at_far(oc)):
+            pl.semaphore_signal(barrier, 1, device_id=dev, device_id_type=MESH)
         return 0
 
     lax.fori_loop(1, PEERS, greet, 0)
+    b_own = core * 8 + x * 2 + zh
+    b_far = core * 8 + x * 2 + 1 - zh
+    e_far = 2 * y + 1 - zh
     rows(gat_a, e, TOK)[...] = nrm_ref[:, :HALF]
-    rows(gat_b, c, TOK)[...] = nrm_ref[:, HALF:]
-    rows(rts_a, e, 16)[...] = own_a[...]
-    rows(rts_b, c, 16)[...] = own_b[...]
-    pl.semaphore_wait(barrier, 2 * (PEERS - 1))
-
-    def spread(i, _):
+    rows(gat_b, b_own, TOK)[...] = nrm_ref[:, HALF:]
+    token = lax.broadcasted_iota(jnp.int32, (TOK, SPAN), 0)
+    lane = lax.broadcasted_iota(jnp.int32, (TOK, SPAN), 1)
+    for rts, index, place in ((rts_a, e, e), (rts_b, b_own, 2 * x + zh)):
+        put = jnp.where(lane == token + place * TOK, 1.0, 0.0)
+        spread = [
+            jnp.dot(a, put, preferred_element_type=F32, precision=lax.Precision.HIGHEST)
+            for a in (ids_ref[...].astype(F32), probs_ref[...])
+        ]
+        rows(rts, index, 16)[...] = jnp.concatenate(spread, axis=0)
+    pl.semaphore_wait(barrier, 3 * (PEERS - 1))
+
+    own_a, own_b = rows(gat_a, e, TOK), rows(gat_b, b_own, TOK)
+    far_a, far_b = rows(gat_a, e_far, TOK), rows(gat_b, b_far, TOK)
+    copy(own_a, own_a, 0, 0, 0, at_z).start()
+    copy(own_b, own_b, 2, 0, 0, at_z).start()
+
+    def routes(i, _):
         oe, oc = lax.rem(e + i, PEERS), lax.rem(c + i, PEERS)
-        push(rts_a, e, rts_a, e, oe, 16, 8, at_exp(oe))
-        push(rts_b, c, rts_b, c, oc, 16, 9, at_ctx(oc))
-        push(gat_a, e, gat_a, e, oe, TOK, 0, at_exp(oe))
-        push(gat_b, c, gat_b, c, oc, TOK, 1, at_ctx(oc))
-        return 0
-
-    lax.fori_loop(1, PEERS, spread, 0)
-    perm = perm_ref[...]
-    for half in range(2):
-        cols = slice(half * 384, half * 384 + 384)
-        at = lax.broadcasted_iota(jnp.int32, (SLOTS, 384), 1) + half * 384
-        pm[:, cols] = jnp.where(perm == at, 1.0, 0.0).astype(BF16)
-    wait_all(rts_a, 16, 8, e)
-    wait_all(rts_b, 16, 9, c)
-    packed_a, packed_b = rts_a[:16, :], rts_b[:16, :]
-    for k in range(1, PEERS):
-        packed_a += rts_a[k * 16:k * 16 + 16, :]
-        packed_b += rts_b[k * 16:k * 16 + 16, :]
-    route_table(packed_a, lambda j: j * PEERS + e, code_a, prob_a, member)
-    route_table(packed_b, lambda j: c * PEERS + j, code_b, prob_b, member)
-    wait_all(gat_a, TOK, 0, e)
-    wait_all(gat_b, TOK, 1, c)
+        mine_a, mine_b = rows(rts_a, e, 16), rows(rts_b, b_own, 16)
+        copy(mine_a, mine_a, 11, oe, e, at_exp(oe)).start()
+        copy(mine_b, mine_b, 12, oc, c, at_ctx(oc)).start()
+        copy(mine_b, mine_b, 13, oc, c, at_far(oc)).start()
+        return 0
+
+    def along(stage, a, b):
+        for i in (1, 3, 2):
+            copy(a, a, stage, i, i, at_y(i)).start()
+            copy(b, b, stage + 2, i, i, at_x(i)).start()
+        copy(b, b, stage + 2, 4, 4, at_sib).start()
+
+    along(0, own_a, own_b)
+    lax.fori_loop(1, PEERS, routes, 0)
+    copy(rows(rts_b, b_own, 16), rows(rts_b, b_own, 16), 13, c, c, at_z).start()
+    same(far_a, 0, 0).wait_recv()
+    same(far_b, 2, 0).wait_recv()
+    along(1, far_a, far_b)
+
+    def order(k, _):
+        part = pl.ds(pl.multiple_of(k * 128, 128), 128)
+        i = lax.broadcasted_iota(jnp.int32, (128, SLOTS), 0) + k * 128
+        at = lax.broadcasted_iota(jnp.int32, (128, SLOTS), 1)
+        ctx = over(i, BLK)
+        rest = i - ctx * BLK
+        oe = over(rest, CAP)
+        oy, ox = over(oe, 2), over(ctx, 2)
+        want = oy * 192 + (ctx - 2 * ox) * BLK + (ox * 2 + oe - 2 * oy) * CAP + rest - oe * CAP
+        pm[part, :] = jnp.where(at == want, 1.0, 0.0).astype(BF16)
+        return 0
+
+    lax.fori_loop(0, SLOTS // 128, order, 0)
+
+    def chip_block(who, i):
+        return rows(gat_b, who * 4 + chip_x(4 - i), 2 * TOK)
+
+    def hand_on(i):
+        for z in range(2):
+            block = rows(gat_b, core * 8 + chip_x(4 - i) * 2 + lax.rem(zh + z, 2), TOK)
+            same(block, 2 + z, i).wait_recv()
+        both = chip_block(core, i)
+        copy(both, both, 4, i, i, at_sib).start()
+
+    hand_on(1)
+    hand_on(3)
+
+    def routes_in(i, _):
+        oe, oc = lax.rem(e + i, PEERS), lax.rem(c + i, PEERS)
+        slot = lax.rem(oc, 2) * 8 + oc // 2 * 2
+        same(rows(rts_a, oe, 16), 11, oe).wait_recv()
+        same(rows(rts_b, slot + zh, 16), 12, oc).wait_recv()
+        same(rows(rts_b, slot + 1 - zh, 16), 13, oc).wait_recv()
+        return 0
+
+    lax.fori_loop(1, PEERS, routes_in, 0)
+    same(rows(rts_b, b_far, 16), 13, c).wait_recv()
+
+    def gathered(rts, first):
+        packed = rts[first * 16:first * 16 + 16, :]
+        for k in range(first + 1, first + PEERS):
+            packed += rts[k * 16:k * 16 + 16, :]
+        return packed
+
+    route_table(gathered(rts_a, 0), lambda j: j * PEERS + e, 0, PEERS, code_a, prob_a, member)
+    rank_table(code_a, member)
+    for k in range(2):
+        route_table(
+            gathered(rts_b, 8 * k), lambda j: c * PEERS + 2 * j + zh, 4 * k, 4, code_b, prob_b, member
+        )
+    rank_table(code_b, member)
+    hand_on(2)
 
     slot_of = lax.broadcasted_iota(jnp.int32, (BLK, SPAN), 0)
 
     def pick(code, index):
         return jnp.where(code[pl.ds(index, 1), :] == slot_of, 1.0, 0.0).astype(BF16)
 
-    def select(code, gat, pair):
-        hot = jnp.concatenate([pick(code, 2 * pair), pick(code, 2 * pair + 1)], axis=0)
-        return jnp.dot(hot, gat[...], preferred_element_type=F32).astype(BF16)
-
-    def route(i, _):
-        pc, pe = lax.rem(c // 2 + i, 4), lax.rem(e // 2 + i, 4)
-        rows(snd_a, pc, 2 * BLK)[...] = select(code_a, gat_a, pc)
+    def select_a(pair):
+        hot = jnp.concatenate([pick(code_a, 2 * pair), pick(code_a, 2 * pair + 1)], axis=0)
+        rows(snd_a, pair, 2 * BLK)[...] = jnp.dot(
+            hot, gat_a[...], preferred_element_type=F32
+        ).astype(BF16)
+
+    def select_b(oy):
         for k in range(2):
-            push(snd_a, 2 * pc + k, arr_a, c, 2 * pc + k, BLK, 2, at_ctx(2 * pc + k))
-        rows(snd_b, pe, 2 * BLK)[...] = select(code_b, gat_b, pe)
+            rows(snd_b, 2 * oy + k, BLK)[...] = jnp.dot(
+                pick(code_b, 4 * k + oy), gat_b[k * SPAN:(k + 1) * SPAN, :], preferred_element_type=F32
+            ).astype(BF16)
+
+    for i in (1, 3, 2):
+        for z in range(2):
+            same(rows(gat_a, 2 * row_y(4 - i) + lax.rem(zh + z, 2), TOK), z, i).wait_recv()
+    first = True
+    for i in (1, 3, 2):
+        oc = chip_x(i)
+        select_a(oc)
         for k in range(2):
-            push(snd_b, 2 * pe + k, arr_b, e, 2 * pe + k, BLK, 3, at_exp(2 * pe + k))
-        return 0
-
-    lax.fori_loop(1, 4, route, 0)
-    pc, pe = c // 2, e // 2
-    sc, se = 2 * pc + 1 - lax.rem(c, 2), 2 * pe + 1 - lax.rem(e, 2)
-    rows(snd_a, pc, 2 * BLK)[...] = select(code_a, gat_a, pc)
-    push(snd_a, sc, arr_a, c, sc, BLK, 2, at_ctx(sc))
-    rows(snd_b, pe, 2 * BLK)[...] = select(code_b, gat_b, pe)
-    push(snd_b, se, arr_b, e, se, BLK, 3, at_exp(se))
+            copy(rows(snd_a, 2 * oc + k, BLK), rows(arr_a, c, BLK), 5, 2 * oc + k, c, at_ctx(2 * oc + k)).start()
+        if first:
+            first = False
+            for z, far in enumerate((zh, 1 - zh)):
+                same(rows(gat_b, (1 - core) * 8 + x * 2 + far, TOK), 2 + z, 4).wait_recv()
+            for k in (1, 3, 2):
+                same(chip_block(1 - core, k), 4, k).wait_recv()
+        oy = row_y(i)
+        select_b(oy)
+        copy(rows(snd_b, oy, 2 * BLK), rows(arr_b, y, 2 * BLK), 6, i, i, at_y(i)).start()
+    select_a(x)
+    copy(rows(snd_a, sib, BLK), rows(arr_a, c, BLK), 5, sib, c, at_sib).start()
+    select_b(y)
     rows(arr_a, c, BLK)[...] = rows(snd_a, c, BLK)[...]
-    rows(arr_b, e, BLK)[...] = rows(snd_b, e, BLK)[...]
+    rows(arr_b, y, 2 * BLK)[...] = rows(snd_b, y, 2 * BLK)[...]
 
     for w in weights:
         w.wait()
-    wait_all(arr_b, BLK, 3, e)
+    for i in (1, 3, 2):
+        same(rows(arr_b, row_y(4 - i), 2 * BLK), 6, i).wait_recv()
 
     def reorder(n, _):
         cols = pl.ds(pl.multiple_of(n * 512, 512), 512)
@@ -182,7 +264,20 @@
         return 0
 
     lax.fori_loop(0, HALF // 512, reorder, 0)
-    wait_all(arr_a, BLK, 2, c)
+
+    def each(ref, size, stage, me, got):
+        def body(i, _):
+            index = lax.rem(me + i, PEERS)
+            w = same(rows(ref, index, size), stage, index)
+            if got:
+                w.wait_recv()
+            else:
+                w.wait_send()
+            return 0
+
+        lax.fori_loop(1, PEERS, body, 0)
+
+    each(arr_a, BLK, 5, c, True)
 
     def hidden_tile(k, _):
         n, m = k // 2, lax.rem(k, 2)
@@ -197,9 +292,12 @@
         return 0
 
     lax.fori_loop(0, 6, hidden_tile, 0)
-    act_b[...] = jnp.dot(pm[...], act[...], preferred_element_type=F32).astype(BF16)
-    sent_all(snd_a, BLK, 2, c)
-    sent_all(snd_b, BLK, 3, e)
+    act_b[...] = lax.dot_general(
+        pm[...], act[...], (((0,), (0,)), ((), ())), preferred_element_type=F32
+    ).astype(BF16)
+    each(snd_a, BLK, 5, c, False)
+    for i in (1, 2, 3):
+        same(rows(snd_b, row_y(i), 2 * BLK), 6, i).wait_send()
 
     def down(src, pair, first, dst):
         part = pl.ds(pl.multiple_of(pair * 2 * BLK, 64), 2 * BLK)
@@ -207,108 +305,129 @@
             src[part, :], wd[:, first:first + HALF], preferred_element_type=F32
         ).astype(BF16)
 
-    def give_back(i, _):
-        pc, pe = lax.rem(c // 2 + i, 4), lax.rem(e // 2 + i, 4)
-        down(act, pc, 0, snd_a)
+    for i in (1, 3, 2):
+        oc, oy = chip_x(i), row_y(i)
+        down(act, oc, 0, snd_a)
         for k in range(2):
-            push(snd_a, 2 * pc + k, ret_a, c, 2 * pc + k, BLK, 4, at_ctx(2 * pc + k))
-        down(act_b, pe, HALF, snd_b)
+            copy(rows(snd_a, 2 * oc + k, BLK), rows(ret_a, c, BLK), 7, 2 * oc + k, c, at_ctx(2 * oc + k)).start()
+        down(act_b, oy, HALF, snd_b)
         for k in range(2):
-            push(snd_b, 2 * pe + k, ret_b, e, 2 * pe + k, BLK, 5, at_exp(2 * pe + k))
-        return 0
-
-    lax.fori_loop(1, 4, give_back, 0)
-    down(act, pc, 0, snd_a)
-    push(snd_a, sc, ret_a, c, sc, BLK, 4, at_ctx(sc))
-    down(act_b, pe, HALF, snd_b)
-    push(snd_b, se, ret_b, e, se, BLK, 5, at_exp(se))
+            copy(
+                rows(snd_b, 2 * oy + k, BLK), rows(ret_b, 4 * k + y, BLK), 8, 4 * k + i, 4 * k + i, at_y(i)
+            ).start()
+    down(act, x, 0, snd_a)
+    copy(rows(snd_a, sib, BLK), rows(ret_a, c, BLK), 7, sib, c, at_sib).start()
+    down(act_b, y, HALF, snd_b)
     rows(ret_a, c, BLK)[...] = rows(snd_a, c, BLK)[...]
-    rows(ret_b, e, BLK)[...] = rows(snd_b, e, BLK)[...]
-
-    def mix(code, prob, ret, prt):
+    for k in range(2):
+        rows(ret_b, 4 * k + y, BLK)[...] = rows(snd_b, 2 * y + k, BLK)[...]
+
+    for stage, a, b in ((0, own_a, own_b), (1, far_a, far_b)):
+        for i in (1, 2, 3):
+            same(a, stage, i).wait_send()
+            same(b, stage + 2, i).wait_send()
+        same(b, stage + 2, 4).wait_send()
+    same(own_a, 0, 0).wait_send()
+    same(own_b, 2, 0).wait_send()
+    for i in (1, 2, 3):
+        same(chip_block(core, i), 4, i).wait_send()
+
+    def mix(code, prob, first, count, ret, prt):
+        size = count * BLK
+        base = first * BLK
+
         def weigh(i, _):
             at = pl.ds(pl.multiple_of(i * BLK, 16), BLK)
             wt[at, :] = jnp.where(
-                code[pl.ds(i, 1), :] == slot_of, prob[pl.ds(i, 1), :], 0.0
+                code[pl.ds(first + i, 1), :] == slot_of, prob[pl.ds(first + i, 1), :], 0.0
             ).astype(BF16)
             return 0
 
-        lax.fori_loop(0, PEERS, weigh, 0)
+        lax.fori_loop(0, count, weigh, 0)
 
         def tile(n, _):
             cols = pl.ds(pl.multiple_of(n * 512, 512), 512)
             prt[:, cols] = lax.dot_general(
-                wt[...], ret[:, cols], (((0,), (0,)), ((), ())), preferred_element_type=F32
+                wt[:size, :], ret[pl.ds(pl.multiple_of(base, 128), size), cols],
+                (((0,), (0,)), ((), ())), preferred_element_type=F32,
             ).astype(BF16)
             return 0
 
         lax.fori_loop(0, HALF // 512, tile, 0)
 
-    wait_all(ret_a, BLK, 4, c)
-    mix(code_a, prob_a, ret_a, prt_a)
-
-    def home_a(i, _):
-        oe = lax.rem(e + i, PEERS)
-        push(prt_a, oe, fin_a, e, oe, TOK, 6, at_exp(oe))
-        return 0
-
-    lax.fori_loop(1, PEERS, home_a, 0)
-    rows(fin_a, e, TOK)[...] = rows(prt_a, e, TOK)[...]
-    wait_all(ret_b, BLK, 5, e)
-    mix(code_b, prob_b, ret_b, prt_b)
-
-    def home_b(i, _):
-        oc = lax.rem(c + i, PEERS)
-        push(prt_b, oc, fin_b, c, oc, TOK, 7, at_ctx(oc))
-        return 0
-
-    lax.fori_loop(1, PEERS, home_b, 0)
-    rows(fin_b, c, TOK)[...] = rows(prt_b, c, TOK)[...]
-
-    wait_all(fin_a, TOK, 6, e)
-    total = hid_ref[:, :HALF]
-    for k in range(PEERS):
-        total += fin_a[k * TOK:(k + 1) * TOK, :].astype(F32)
-    out_ref[:, :HALF] = total.astype(BF16)
-    wait_all(fin_b, TOK, 7, c)
-    total = hid_ref[:, HALF:]
-    for k in range(PEERS):
-        total += fin_b[k * TOK:(k + 1) * TOK, :].astype(F32)
-    out_ref[:, HALF:] = total.astype(BF16)
-
-    sent_all(gat_a, TOK, 0, e)
-    sent_all(gat_b, TOK, 1, c)
-    sent_all(snd_a, BLK, 4, c)
-    sent_all(snd_b, BLK, 5, e)
-    sent_all(prt_a, TOK, 6, e)
-    sent_all(prt_b, TOK, 7, c)
-    sent_all(rts_a, 16, 8, e)
-    sent_all(rts_b, 16, 9, c)
-
-
-def moe(hidden, normed, own_a, own_b, w_gate, w_up, w_down):
-    i = lax.iota(jnp.int32, SLOTS)
-    perm = (i % BLK // CAP * BLK + i // BLK * CAP + i % CAP)[:, None]
+    for i in (1, 3, 2):
+        for k in range(2):
+            same(rows(ret_b, 4 * k + row_y(4 - i), BLK), 8, 4 * k + i).wait_recv()
+    sib_half, own_half = rows(gat_b, 1 - core, SPAN), rows(gat_b, core, SPAN)
+    mix(code_b, prob_b, 4 * (1 - core), 4, ret_b, sib_half)
+    copy(sib_half, sib_b, 10, 0, 0, at_sib).start()
+    mix(code_b, prob_b, 4 * core, 4, ret_b, own_half)
+    same(sib_b, 10, 0).wait_recv()
+
+    def add_sib(k, _):
+        at = pl.ds(pl.multiple_of(k * 2 * TOK, 32), 2 * TOK)
+        own_half[at, :] = (own_half[at, :].astype(F32) + sib_b[at, :].astype(F32)).astype(BF16)
+        return 0
+
+    lax.fori_loop(0, 4, add_sib, 0)
+    for i in (1, 3, 2):
+        copy(rows(own_half, chip_x(i), 2 * TOK), rows(fin_b, i - 1, 2 * TOK), 10, i, i, at_x(i)).start()
+    each(ret_a, BLK, 7, c, True)
+    mix(code_a, prob_a, 0, PEERS, ret_a, gat_a)
+    for i in (1, 3, 2):
+        copy(rows(gat_a, row_y(i), 2 * TOK), rows(fin_a, i - 1, 2 * TOK), 9, i, i, at_y(i)).start()
+
+    def home(k, part, fin, stage, zsem):
+        for i in (1, 3, 2):
+            same(rows(fin, i - 1, 2 * TOK), stage, i).wait_recv()
+        tot[...] = part[...].astype(F32)
+        for i in range(3):
+            tot[...] += rows(fin, i, 2 * TOK)[...].astype(F32)
+        rows(zed, k, TOK)[...] = rows(tot, 1 - zh, TOK)[...].astype(BF16)
+        copy(rows(zed, k, TOK), rows(zin, k, TOK), stage, zsem, zsem, at_z).start()
+        rows(keep, k, TOK)[...] = hid_ref[:, k * HALF:(k + 1) * HALF] + rows(tot, zh, TOK)[...]
+
+    home(1, rows(own_half, x, 2 * TOK), fin_b, 10, 4)
+    home(0, rows(gat_a, y, 2 * TOK), fin_a, 9, 0)
+    same(rows(zin, 1, TOK), 10, 4).wait_recv()
+    out_ref[:, HALF:] = (keep[TOK:, :] + zin[TOK:, :].astype(F32)).astype(BF16)
+    same(rows(zin, 0, TOK), 9, 0).wait_recv()
+    out_ref[:, :HALF] = (keep[:TOK, :] + zin[:TOK, :].astype(F32)).astype(BF16)
+
+    each(snd_a, BLK, 7, c, False)
+    for i in (1, 2, 3):
+        for k in range(2):
+            same(rows(snd_b, 2 * row_y(i) + k, BLK), 8, 4 * k + i).wait_send()
+        same(rows(own_half, chip_x(i), 2 * TOK), 10, i).wait_send()
+        same(rows(gat_a, row_y(i), 2 * TOK), 9, i).wait_send()
+    same(sib_half, 10, 0).wait_send()
+    same(rows(zed, 1, TOK), 10, 4).wait_send()
+    same(rows(zed, 0, TOK), 9, 0).wait_send()
+
+    def routes_out(i, _):
+        oe, oc = lax.rem(e + i, PEERS), lax.rem(c + i, PEERS)
+        same(rows(rts_a, e, 16), 11, oe).wait_send()
+        same(rows(rts_b, b_own, 16), 12, oc).wait_send()
+        same(rows(rts_b, b_own, 16), 13, oc).wait_send()
+        return 0
+
+    lax.fori_loop(1, PEERS, routes_out, 0)
+    same(rows(rts_b, b_own, 16), 13, c).wait_send()
+
+
+def moe(hidden, normed, ids, probs, w_gate, w_up, w_down):
     vm = pl.BlockSpec(memory_space=pltpu.VMEM)
     hbm = pl.BlockSpec(memory_space=pl.ANY)
+    half = [(SPAN, HALF), (2 * SPAN, HALF)] + [(SLOTS, HALF)] * 6 + [(6 * TOK, HALF)] * 2
+    half += [(SPAN, HALF), (2 * TOK, HALF), (2 * TOK, HALF)]
     return pl.pallas_call(
         moe_kernel,
         out_shape=jax.ShapeDtypeStruct((TOK, D), BF16),
-        in_specs=[vm] * 5 + [hbm] * 3,
+        in_specs=[vm] * 4 + [hbm] * 3,
         out_specs=vm,
-        scratch_shapes=[
-            pltpu.VMEM((SPAN, HALF), BF16),
-            pltpu.VMEM((SPAN, HALF), BF16),
-            pltpu.VMEM((SLOTS, HALF), BF16),
-            pltpu.VMEM((SLOTS, HALF), BF16),
-            pltpu.VMEM((SLOTS, HALF), BF16),
-            pltpu.VMEM((SLOTS, HALF), BF16),
-            pltpu.VMEM((SLOTS, HALF), BF16),
-            pltpu.VMEM((SLOTS, HALF), BF16),
-            pltpu.VMEM((SPAN, HALF), BF16),
-            pltpu.VMEM((SPAN, HALF), BF16),
-            pltpu.VMEM((SPAN, HALF), BF16),
-            pltpu.VMEM((SPAN, HALF), BF16),
+        scratch_shapes=[pltpu.VMEM(shape, BF16) for shape in half] + [
+            pltpu.VMEM((2 * TOK, HALF), F32),
+            pltpu.VMEM((2 * TOK, HALF), F32),
             pltpu.VMEM((SLOTS, HALF), BF16),
             pltpu.VMEM((SLOTS, FF), BF16),
             pltpu.VMEM((SLOTS, FF), BF16),
@@ -318,28 +437,28 @@
             pltpu.VMEM((D, FF), BF16),
             pltpu.VMEM((FF, D), BF16),
             pltpu.VMEM((PEERS * 16, SPAN), F32),
-            pltpu.VMEM((PEERS * 16, SPAN), F32),
+            pltpu.VMEM((2 * PEERS * 16, SPAN), F32),
             pltpu.VMEM((PEERS, SPAN), jnp.int32),
             pltpu.VMEM((PEERS, SPAN), jnp.int32),
             pltpu.VMEM((PEERS, SPAN), F32),
             pltpu.VMEM((PEERS, SPAN), F32),
             pltpu.VMEM((PEERS, SPAN), F32),
             pltpu.SemaphoreType.DMA((3,)),
-            pltpu.SemaphoreType.DMA((10, PEERS)),
-            pltpu.SemaphoreType.DMA((10, PEERS)),
+            pltpu.SemaphoreType.DMA((14, PEERS)),
+            pltpu.SemaphoreType.DMA((14, PEERS)),
         ],
         compiler_params=pltpu.CompilerParams(
             collective_id=1, has_side_effects=True, vmem_limit_bytes=62 * 1024 * 1024
         ),
-        cost_estimate=pl.CostEstimate(flops=18_000_000_000, bytes_accessed=20_000_000, transcendentals=600_000),
+        cost_estimate=pl.CostEstimate(flops=20_000_000_000, bytes_accessed=20_000_000, transcendentals=600_000),
         name="moe",
-    )(hidden, normed, own_a, own_b, perm, w_gate, w_up, w_down)
+    )(hidden, normed, ids, probs, w_gate, w_up, w_down)
 
 
 def attn_kernel(
-    off_ref, q_ref, k_hbm, v_hbm, w_hbm, res_ref, gain_ref,
+    off_ref, q_hbm, k_hbm, v_hbm, w_hbm, res_hbm, gain_hbm,
     hid_ref, nrm_ref,
-    kv, wbuf, mx, acc, att, pbuf, rbuf, tot, zsnd, zbuf,
+    q_ref, res_ref, gain_ref, kv, wbuf, mx, acc, att, pbuf, rbuf, tot, zsnd, zbuf,
     l_sem, kv_s, kv_r, w_s, w_r, y_s, y_r, z_s, z_r,
 ):
     dp, c, e = lax.axis_index("dp"), lax.axis_index("ctx"), lax.axis_index("exp")
@@ -370,6 +489,9 @@
         pltpu.make_async_copy(k_hbm.at[:, cols], own.at[:, :HD], l_sem.at[0]),
         pltpu.make_async_copy(v_hbm.at[:, cols], own.at[:, HD:], l_sem.at[1]),
         pltpu.make_async_copy(w_hbm, rows(wbuf, c, HEADS), l_sem.at[2]),
+        pltpu.make_async_copy(q_hbm, q_ref, l_sem.at[3]),
+        pltpu.make_async_copy(res_hbm, res_ref, l_sem.at[4]),
+        pltpu.make_async_copy(gain_hbm, gain_ref, l_sem.at[5]),
     ]
     for load in loads:
         load.start()
@@ -450,12 +572,14 @@
 
         lax.fori_loop(0, 8, head, 0)
 
+    loads[2].wait()
+    w_to_sib.start()
+    for i in (1, 3, 2):
+        w_direct(i).start()
+    for load in loads[3:]:
+        load.wait()
     k_from_sib.wait_recv()
     group(0)
-    loads[2].wait()
-    w_to_sib.start()
-    for i in (1, 3, 2):
-        w_direct(i).start()
     for i in (1, 3):
         k_arrival(i).wait_recv()
         k_handed(i).start()
@@ -566,9 +690,12 @@
     return pl.pallas_call(
         attn_kernel,
         out_shape=(jax.ShapeDtypeStruct((TOK, D), F32), jax.ShapeDtypeStruct((TOK, D), BF16)),
-        in_specs=[pl.BlockSpec(memory_space=pltpu.SMEM), vm, hbm, hbm, hbm, vm, vm],
+        in_specs=[pl.BlockSpec(memory_space=pltpu.SMEM)] + [hbm] * 6,
         out_specs=(vm, vm),
         scratch_shapes=[
+            pltpu.VMEM((SPAN, HEADS), BF16),
+            pltpu.VMEM((TOK, D), BF16),
+            pltpu.VMEM((1, D), F32),
             pltpu.VMEM((PEERS * SPAN, 2 * HD), BF16),
             pltpu.VMEM((PEERS * HEADS, 512), BF16),
             pltpu.VMEM((8 * SPAN, HD), F32),
@@ -579,11 +706,11 @@
             pltpu.VMEM((2 * TOK, 512), F32),
             pltpu.VMEM((PEERS * TOK, 512), BF16),
             pltpu.VMEM((PEERS * TOK, 512), BF16),
-            dma((3,)), dma((7,)), dma((7,)), dma((7,)), dma((7,)),
+            dma((6,)), dma((7,)), dma((7,)), dma((7,)), dma((7,)),
             dma((PEERS, 3)), dma((PEERS, 3)), dma((PEERS,)), dma((PEERS,)),
         ],
         compiler_params=pltpu.CompilerParams(
-            collective_id=2, has_side_effects=True, vmem_limit_bytes=48 * 1024 * 1024
+            collective_id=2, has_side_effects=True, vmem_limit_bytes=62 * 1024 * 1024
         ),
         cost_estimate=pl.CostEstimate(flops=9_000_000_000, bytes_accessed=4_000_000, transcendentals=10_000_000),
         name="attend",
@@ -593,13 +720,8 @@
 def shards(
     queries, keys, values, offsets, out_proj, residual, norm_gain, expert_ids, gate_probs, w_gate, w_up, w_down,
 ):
-    packed = jnp.concatenate([expert_ids.T.astype(F32), gate_probs.T], axis=0)
-    tiled = jnp.tile(packed, (1, PEERS))
-    block = lax.iota(jnp.int32, SPAN) // TOK
-    own_a = jnp.where(block == lax.axis_index("exp"), tiled, 0.0)
-    own_b = jnp.where(block == lax.axis_index("ctx"), tiled, 0.0)
     hidden, normed = attend(offsets, queries, keys, values, out_proj, residual, norm_gain[None, :])
-    return moe(hidden, normed, own_a, own_b, w_gate, w_up, w_down)
+    return moe(hidden, normed, expert_ids.T, gate_probs.T, w_gate, w_up, w_down)
 
 
 def solution(mesh):

time: 253 us -> 248 us (0.980); the launches traced: 249 us -> 247 us
  Pallas kernels: 236 us -> 245 us
  local copies, waits for them, and re-layouts: 10.2 us -> 1.77 us
  other arithmetic: 3.32 us -> 0 us
    unnamed x19 -> x1, local copies, waits for them, and re-layouts: 10.1 us -> 1.77 us
    pallas_call x1, Pallas kernels: 153 us -> 162 us  [moe(): pl.pallas_call(moe_kernel, out_shape=jax.ShapeDtypeStruct((TOK, D), BF16)...]
where the time goes in v3:
time: 248 us; the launch traced here: 247 us
  Pallas kernels  245 us (99%)
    pallas_call x1, Pallas kernels, moe(): pl.pallas_call(moe_kernel, out_shape=jax.ShapeDtypeStruct((TOK, D), BF16)...  162 us
    pallas_call x1, Pallas kernels, attend(): pl.pallas_call(attn_kernel, out_shape=(jax.ShapeDtypeStruct((TOK, D), F32...  83.8 us

profile of v3, /device:TPU:1, one launch (start us, length us, event | category | flops | bytes accessed | tf_op | source)
XLA Modules:
  0.0 247.3 jit_solution(458527287493004604)
XLA Ops:
  0.0 83.8 %attend.1 = (f32[48,4096]{1,0:T(8,128)}, bf16[48,4096]{1,0:T(8,128)(2,1)}) custom-call(s32[8]{0:T(128)} %off_ref.1, bf16[384,1024]{1,0:T(8,128)(2,1)} %q_hbm.1, bf16[384,512]{1,0:T(8,128)(2,1)} %k_hbm.1, bf16[384,512]{1,0:T(8,128)(2,1)} %v_hbm.1, bf16[1024,512]{1,0:T(8,128)(2,1)} %w_hbm.1, bf16[48,4096]{1,0:T(8,128)(2,1)} %res_hbm.1, f32[1,4096]{1,0:T(1,128)} %bitcast.3), custom_call_target="tpu_custom_call" | custom-call | flops 8999999488 | bytes 4000000 | tf_op jit(solution)/shard_map/attend/pallas_call | solution.py:690
  83.8 161.7 %moe.1 = bf16[48,4096]{1,0:T(8,128)(2,1)} custom-call(f32[48,4096]{1,0:T(8,128)} %get-tuple-element.7.hid_ref, bf16[48,4096]{1,0:T(8,128)(2,1)} %get-tuple-element.8.nrm_ref, s32[8,48]{1,0:T(8,128)} %bitcast.4, f32[8,48]{1,0:T(8,128)} %bitcast.5, bf16[1,4096,768]{2,1,0:T(8,128)(2,1)} %wg_hbm.1, bf16[1,4096,768]{2,1,0:T(8,128)(2,1)} %wu_hbm.1, ...), custom_call_target="tpu_custom_call" | custom-call | flops 20000000000 | bytes 20000000 | tf_op jit(solution)/shard_map/moe/pallas_call | solution.py:423
  245.5 1.8 copy.14

commit v4 on v3

v4 whole, which is shorter than its diff:
```python
import math

import jax
import jax.numpy as jnp
from jax import lax
from jax.experimental import pallas as pl
from jax.experimental.pallas import tpu as pltpu
from jax.sharding import PartitionSpec as P

KVH = 4
HD = 128
D = 4096
HALF = D // 2
FF = 768
TOK = 48
CAP = 12
PEERS = 8
BLK = PEERS * CAP
SLOTS = PEERS * BLK
SPAN = PEERS * TOK
HEADS = 8 * HD

NEG_FILL = -1e30
MESH = pl.DeviceIdType.MESH
F32 = jnp.float32
BF16 = jnp.bfloat16


def over(a, n):
    return ((a.astype(F32) + 0.5) * (1.0 / n)).astype(jnp.int32)


def route_table(packed, expert_of, count, code, prob, member):
    ids, probs = packed[:8], packed[8:]
    width = packed.shape[1]
    for j in range(count):
        named = ids == expert_of(j).astype(F32)
        member[j:j + 1, :] = jnp.sum(jnp.where(named, 1.0, 0.0), axis=0, keepdims=True)
        prob[j:j + 1, :] = jnp.sum(jnp.where(named, probs, 0.0), axis=0, keepdims=True)
    before = lax.broadcasted_iota(jnp.int32, (width, width), 0)
    t = lax.broadcasted_iota(jnp.int32, (width, width), 1)
    block = over(t, TOK)
    earlier = jnp.where((before < t) & (before >= block * TOK), 1.0, 0.0).astype(BF16)
    inside = member[...]
    rank = jnp.dot(inside.astype(BF16), earlier, preferred_element_type=F32)
    code[...] = jnp.where(inside > 0.5, block[:8] * CAP + rank.astype(jnp.int32), -1)


def moe_kernel(
    hid_ref, nrm_ref, ids_ref, probs_ref, wg_hbm, wu_hbm, wd_hbm,
    out_ref,
    gat_a, gat_b, snd_a, snd_b, arr_a, arr_b, ret_a, ret_b, fin_a, fin_b, sib_b, zed, zin,
    xb, act, act_b, pm, wt_a, wt_b, wg, wu, wd,
    rts_a, rts_b, code_a, code_b, prob_a, prob_b, member_a, member_b, keep,
    w_sem, s_sem, r_sem,
):
    dp, c, e = lax.axis_index("dp"), lax.axis_index("ctx"), lax.axis_index("exp")
    x, core, y, zh = c // 2, lax.rem(c, 2), e // 2, lax.rem(e, 2)
    v = lax.rem(dp + e, 2)
    sib = 2 * x + 1 - core
    place_b = core * 4 + x

    def at_exp(other):
        return (lax.rem(v + other, 2), c, other)

    def at_ctx(other):
        return (dp, other, e)

    def at_far(other):
        return (1 - dp, other, 2 * y + 1 - zh)

    def chip_x(i):
        return lax.rem(x + i, 4)

    def at_x(i):
        return (dp, 2 * chip_x(i) + core, e)

    def row_y(i):
        return lax.rem(y + i, 4)

    def at_y(i):
        return (dp, c, 2 * row_y(i) + zh)

    at_sib = (dp, sib, e)
    at_z = at_far(c)

    weights = [
        pltpu.make_async_copy(src.at[0], dst, w_sem.at[i])
        for i, (src, dst) in enumerate(((wg_hbm, wg), (wu_hbm, wu), (wd_hbm, wd)))
    ]
    for w in weights:
        w.start()

    def rows(ref, index, size):
        return ref.at[pl.ds(pl.multiple_of(index * size, 16), size)]

    def copy(src, dst, stage, sent, got, dev):
        return pltpu.make_async_remote_copy(
            src_ref=src, dst_ref=dst, send_sem=s_sem.at[stage, sent], recv_sem=r_sem.at[stage, got],
            device_id=dev, device_id_type=MESH,
        )

    def same(ref, stage, index):
        return copy(ref, ref, stage, index, index, at_sib)

    def block_a(q, oy):
        return rows(gat_a, 4 * q + oy, TOK)

    def block_b(q, who, ox):
        return rows(gat_b, 8 * q + 4 * who + ox, TOK)

    barrier = pltpu.get_barrier_semaphore()

    def greet(i, _):
        oe, oc = lax.rem(e + i, PEERS), lax.rem(c + i, PEERS)
        for dev in (at_exp(oe), at_ctx(oc), at_far(oc)):
            pl.semaphore_signal(barrier, 1, device_id=dev, device_id_type=MESH)
        return 0

    lax.fori_loop(1, PEERS, greet, 0)
    block_a(0, y)[...] = nrm_ref[:, :HALF]
    block_b(0, core, x)[...] = nrm_ref[:, HALF:]
    pl.semaphore_wait(barrier, 3 * (PEERS - 1))

    def along(q):
        a, b = block_a(q, y), block_b(q, core, x)
        for i in (1, 3, 2):
            copy(a, a, q, i, i, at_y(i)).start()
            copy(b, b, 2 + q, i, i, at_x(i)).start()
        copy(b, b, 2 + q, 4, 4, at_sib).start()

    copy(block_a(0, y), block_a(1, y), 18, 0, 0, at_z).start()
    copy(block_b(0, core, x), block_b(1, core, x), 18, 1, 1, at_z).start()
    along(0)
    for rts, index, place, width in ((rts_a, y, y, 4 * TOK), (rts_b, place_b, place_b, SPAN)):
        token = lax.broadcasted_iota(jnp.int32, (TOK, width), 0)
        lane = lax.broadcasted_iota(jnp.int32, (TOK, width), 1)
        put = jnp.where(lane == token + place * TOK, 1.0, 0.0)
        spread = [
            jnp.dot(a, put, preferred_element_type=F32, precision=lax.Precision.HIGHEST)
            for a in (ids_ref[...].astype(F32), probs_ref[...])
        ]
        rows(rts, index, 16)[...] = jnp.concatenate(spread, axis=0)

    def slot_e(oe):
        far = lax.rem(oe + e, 2)
        return 4 * far + oe // 2, 4 * far + y

    def routes(i, _):
        oe, oc = lax.rem(e + i, PEERS), lax.rem(c + i, PEERS)
        _, mine = slot_e(oe)
        copy(rows(rts_a, y, 16), rows(rts_a, mine, 16), 19, i, mine, at_exp(oe)).start()
        own = rows(rts_b, place_b, 16)
        copy(own, own, 20, i, place_b, at_ctx(oc)).start()
        copy(own, rows(rts_b, 8 + place_b, 16), 21, i, place_b, at_far(oc)).start()
        return 0

    lax.fori_loop(1, PEERS, routes, 0)
    copy(rows(rts_b, place_b, 16), rows(rts_b, 8 + place_b, 16), 21, 0, place_b, at_z).start()
    same(block_a(1, y), 18, 0).wait_recv()
    same(block_b(1, core, x), 18, 1).wait_recv()
    along(1)

    i = lax.broadcasted_iota(jnp.int32, (4 * BLK, 4 * BLK), 0)
    at = lax.broadcasted_iota(jnp.int32, (4 * BLK, 4 * BLK), 1)
    from_c = over(i, TOK)
    rest = i - from_c * TOK
    from_y = over(rest, CAP)
    from_x = over(from_c, 2)
    want = from_y * BLK + ((from_c - 2 * from_x) * 4 + from_x) * CAP + rest - from_y * CAP
    pm[...] = jnp.where(at == want, 1.0, 0.0).astype(BF16)

    def hand_on(q, i):
        block = block_b(q, core, chip_x(4 - i))
        same(block, 2 + q, i).wait_recv()
        copy(block, block, 4 + q, i, i, at_sib).start()

    hand_on(0, 1)
    hand_on(0, 3)

    def routes_in(i, _):
        oe, oc = lax.rem(e + i, PEERS), lax.rem(c + i, PEERS)
        theirs, _ = slot_e(oe)
        same(rows(rts_a, theirs, 16), 19, theirs).wait_recv()
        other = lax.rem(oc, 2) * 4 + oc // 2
        same(rows(rts_b, other, 16), 20, other).wait_recv()
        same(rows(rts_b, 8 + other, 16), 21, other).wait_recv()
        return 0

    lax.fori_loop(1, PEERS, routes_in, 0)
    same(rows(rts_b, 8 + place_b, 16), 21, place_b).wait_recv()
    hand_on(0, 2)

    def gathered(rts, first, count):
        packed = rts[first * 16:first * 16 + 16, :]
        for k in range(first + 1, first + count):
            packed += rts[k * 16:k * 16 + 16, :]
        return packed

    member_b[...] = jnp.zeros_like(member_b)
    for q in range(2):
        route_table(
            gathered(rts_a, 4 * q, 4), lambda j: j * PEERS + e, PEERS, code_a.at[q], prob_a.at[q], member_a
        )
        route_table(
            gathered(rts_b, 8 * q, 8), lambda j: c * PEERS + 2 * j + zh, 4, code_b.at[q], prob_b.at[q], member_b
        )
    for i in (1, 3, 2):
        hand_on(1, i)

    slot_a = lax.broadcasted_iota(jnp.int32, (TOK, 4 * TOK), 0)
    slot_b = lax.broadcasted_iota(jnp.int32, (BLK, SPAN), 0)

    def select(q):
        for k in range(PEERS):
            wt_a[k * TOK:(k + 1) * TOK, :] = jnp.where(
                code_a[q, k:k + 1, :] == slot_a, 1.0, 0.0
            ).astype(BF16)
        for k in range(4):
            wt_b[k * BLK:(k + 1) * BLK, :] = jnp.where(
                code_b[q, k:k + 1, :] == slot_b, 1.0, 0.0
            ).astype(BF16)
        part = slice(q * SPAN, q * SPAN + SPAN)

        def tile(n, _):
            cols = pl.ds(pl.multiple_of(n * 512, 512), 512)
            snd_a[part, cols] = jnp.dot(
                wt_a[...], gat_a[q * 4 * TOK:(q + 1) * 4 * TOK, cols], preferred_element_type=F32
            ).astype(BF16)
            snd_b[part, cols] = jnp.dot(
                wt_b[...], gat_b[part, cols], preferred_element_type=F32
            ).astype(BF16)
            return 0

        lax.fori_loop(0, HALF // 512, tile, 0)

    def exchange(q, dst_a, dst_b, stage):
        for i in (1, 3, 2):
            for k in range(2):
                oc = 2 * chip_x(i) + k
                copy(
                    rows(snd_a, 8 * q + oc, TOK), rows(dst_a, 8 * q + c, TOK), stage + q, oc, c, at_ctx(oc)
                ).start()
            copy(
                rows(snd_b, 4 * q + row_y(i), BLK), rows(dst_b, 4 * q + y, BLK), stage + 2 + q, i, i, at_y(i)
            ).start()
        copy(rows(snd_a, 8 * q + sib, TOK), rows(dst_a, 8 * q + c, TOK), stage + q, sib, c, at_sib).start()
        rows(dst_a, 8 * q + c, TOK)[...] = rows(snd_a, 8 * q + c, TOK)[...]
        rows(dst_b, 4 * q + y, BLK)[...] = rows(snd_b, 4 * q + y, BLK)[...]

    def exchange_in(q, dst_a, dst_b, stage):
        for i in (1, 3, 2):
            same(rows(dst_b, 4 * q + row_y(4 - i), BLK), stage + 2 + q, i).wait_recv()

        def body(i, _):
            oc = lax.rem(c + i, PEERS)
            same(rows(dst_a, 8 * q + oc, TOK), stage + q, oc).wait_recv()
            return 0

        lax.fori_loop(1, PEERS, body, 0)

    def exchange_out(q, stage):
        for i in (1, 3, 2):
            same(rows(snd_b, 4 * q + row_y(i), BLK), stage + 2 + q, i).wait_send()

        def body(i, _):
            oc = lax.rem(c + i, PEERS)
            same(rows(snd_a, 8 * q + oc, TOK), stage + q, oc).wait_send()
            return 0

        lax.fori_loop(1, PEERS, body, 0)

    for q in (1, 0):
        for i in (1, 3, 2):
            same(block_a(q, row_y(4 - i)), q, i).wait_recv()
            same(block_b(q, 1 - core, chip_x(4 - i)), 4 + q, i).wait_recv()
        same(block_b(q, 1 - core, x), 2 + q, 4).wait_recv()
        select(q)
        if q == 0:
            exchange_out(1, 6)
        exchange(q, arr_a, arr_b, 6)

    for w in weights:
        w.wait()

    def experts(q):
        part = slice(q * SPAN, q * SPAN + SPAN)

        def reorder(n, _):
            cols = pl.ds(pl.multiple_of(n * 512, 512), 512)
            xb[:, cols] = jnp.dot(pm[...], arr_b[part, cols], preferred_element_type=F32).astype(BF16)
            return 0

        lax.fori_loop(0, HALF // 512, reorder, 0)

        def hidden_tile(n, _):
            cols = pl.ds(pl.multiple_of(n * 256, 256), 256)
            a, b = arr_a[part, :], xb[...]
            gate = jnp.dot(a, wg[:HALF, cols], preferred_element_type=F32)
            gate += jnp.dot(b, wg[HALF:, cols], preferred_element_type=F32)
            up = jnp.dot(a, wu[:HALF, cols], preferred_element_type=F32)
            up += jnp.dot(b, wu[HALF:, cols], preferred_element_type=F32)
            act[:, cols] = (gate / (1.0 + jnp.exp(-gate)) * up).astype(BF16)
            return 0

        lax.fori_loop(0, FF // 256, hidden_tile, 0)
        act_b[...] = lax.dot_general(
            pm[...], act[...], (((0,), (0,)), ((), ())), preferred_element_type=F32
        ).astype(BF16)

        def down(n, _):
            cols = pl.ds(pl.multiple_of(n * 512, 512), 512)
            late = pl.ds(pl.multiple_of(n * 512 + HALF, 512), 512)
            snd_a[part, cols] = jnp.dot(act[...], wd[:, cols], preferred_element_type=F32).astype(BF16)
            snd_b[part, cols] = jnp.dot(act_b[...], wd[:, late], preferred_element_type=F32).astype(BF16)
            return 0

        lax.fori_loop(0, HALF // 512, down, 0)

    for q in (1, 0):
        exchange_in(q, arr_a, arr_b, 6)
        if q == 0:
            exchange_out(0, 6)
        experts(q)
        exchange(q, ret_a, ret_b, 10)

    for q in range(2):
        for i in (1, 2, 3):
            same(block_a(q, y), q, i).wait_send()
            same(block_b(q, core, x), 2 + q, i).wait_send()
            same(block_b(q, core, x), 4 + q, i).wait_send()
        same(block_b(q, core, x), 2 + q, 4).wait_send()
    same(block_a(0, y), 18, 0).wait_send()
    same(block_b(0, core, x), 18, 1).wait_send()

    def half_b(q, who):
        return rows(gat_b, 2 * q + who, 4 * TOK)

    def mix(q):
        for k in range(PEERS):
            wt_a[k * TOK:(k + 1) * TOK, :] = jnp.where(
                code_a[q, k:k + 1, :] == slot_a, prob_a[q, k:k + 1, :], 0.0
            ).astype(BF16)
        for k in range(4):
            wt_b[k * BLK:(k + 1) * BLK, :] = jnp.where(
                code_b[q, k:k + 1, :] == slot_b, prob_b[q, k:k + 1, :], 0.0
            ).astype(BF16)
        part = slice(q * SPAN, q * SPAN + SPAN)

        def tile_b(n, _):
            cols = pl.ds(pl.multiple_of(n * 512, 512), 512)
            gat_b[part, cols] = lax.dot_general(
                wt_b[...], ret_b[part, cols], (((0,), (0,)), ((), ())), preferred_element_type=F32
            ).astype(BF16)
            return 0

        def tile_a(n, _):
            cols = pl.ds(pl.multiple_of(n * 512, 512), 512)
            gat_a[q * 4 * TOK:(q + 1) * 4 * TOK, cols] = lax.dot_general(
                wt_a[...], ret_a[part, cols], (((0,), (0,)), ((), ())), preferred_element_type=F32
            ).astype(BF16)
            return 0

        lax.fori_loop(0, HALF // 512, tile_b, 0)
        copy(half_b(q, 1 - core), rows(sib_b, q, 4 * TOK), 16 + q, 0, 0, at_sib).start()
        lax.fori_loop(0, HALF // 512, tile_a, 0)
        for i in (1, 3, 2):
            copy(block_a(q, row_y(i)), rows(fin_a, 3 * q + i - 1, TOK), 14 + q, i, i, at_y(i)).start()
        same(rows(sib_b, q, 4 * TOK), 16 + q, 0).wait_recv()
        for i in (1, 3, 2, 0):
            own = block_b(q, core, chip_x(i))
            own[...] = (
                own[...].astype(F32) + rows(sib_b, 4 * q + chip_x(i), TOK)[...].astype(F32)
            ).astype(BF16)
            if i:
                copy(own, rows(fin_b, 3 * q + i - 1, TOK), 16 + q, i, i, at_x(i)).start()

    for q in (1, 0):
        exchange_in(q, ret_a, ret_b, 10)
        mix(q)

    def home(q, own, fin, stage):
        total = own[...].astype(F32)
        for i in (1, 3, 2):
            same(rows(fin, 3 * q + i - 1, TOK), stage + q, i).wait_recv()
        for i in range(3):
            total += rows(fin, 3 * q + i, TOK)[...].astype(F32)
        return total

    zed[:TOK, :] = home(1, block_a(1, y), fin_a, 14).astype(BF16)
    copy(zed.at[:TOK], zin.at[:TOK], 18, 2, 2, at_z).start()
    zed[TOK:, :] = home(1, block_b(1, core, x), fin_b, 16).astype(BF16)
    copy(zed.at[TOK:], zin.at[TOK:], 18, 3, 3, at_z).start()
    keep[:TOK, :] = hid_ref[:, :HALF] + home(0, block_a(0, y), fin_a, 14)
    keep[TOK:, :] = hid_ref[:, HALF:] + home(0, block_b(0, core, x), fin_b, 16)
    same(zin.at[:TOK], 18, 2).wait_recv()
    out_ref[:, :HALF] = (keep[:TOK, :] + zin[:TOK, :].astype(F32)).astype(BF16)
    same(zin.at[TOK:], 18, 3).wait_recv()
    out_ref[:, HALF:] = (keep[TOK:, :] + zin[TOK:, :].astype(F32)).astype(BF16)

    same(zed.at[:TOK], 18, 2).wait_send()
    same(zed.at[TOK:], 18, 3).wait_send()
    for q in range(2):
        exchange_out(q, 10)
        for i in (1, 2, 3):
            same(block_a(q, row_y(i)), 14 + q, i).wait_send()
            same(block_b(q, core, chip_x(i)), 16 + q, i).wait_send()
        same(half_b(q, 1 - core), 16 + q, 0).wait_send()

    def routes_out(i, _):
        same(rows(rts_a, y, 16), 19, i).wait_send()
        same(rows(rts_b, place_b, 16), 20, i).wait_send()
        same(rows(rts_b, place_b, 16), 21, i).wait_send()
        return 0

    lax.fori_loop(1, PEERS, routes_out, 0)
    same(rows(rts_b, place_b, 16), 21, 0).wait_send()


def moe(hidden, normed, ids, probs, w_gate, w_up, w_down):
    vm = pl.BlockSpec(memory_space=pltpu.VMEM)
    hbm = pl.BlockSpec(memory_space=pl.ANY)
    half = [8 * TOK, 16 * TOK] + [SLOTS] * 6 + [6 * TOK, 6 * TOK, 8 * TOK, 2 * TOK, 2 * TOK, SPAN]
    return pl.pallas_call(
        moe_kernel,
        out_shape=jax.ShapeDtypeStruct((TOK, D), BF16),
        in_specs=[vm] * 4 + [hbm] * 3,
        out_specs=vm,
        scratch_shapes=[pltpu.VMEM((n, HALF), BF16) for n in half] + [
            pltpu.VMEM((SPAN, FF), BF16),
            pltpu.VMEM((SPAN, FF), BF16),
            pltpu.VMEM((4 * BLK, 4 * BLK), BF16),
            pltpu.VMEM((PEERS * TOK, 4 * TOK), BF16),
            pltpu.VMEM((4 * BLK, SPAN), BF16),
            pltpu.VMEM((D, FF), BF16),
            pltpu.VMEM((D, FF), BF16),
            pltpu.VMEM((FF, D), BF16),
            pltpu.VMEM((PEERS * 16, 4 * TOK), F32),
            pltpu.VMEM((2 * PEERS * 16, SPAN), F32),
            pltpu.VMEM((2, PEERS, 4 * TOK), jnp.int32),
            pltpu.VMEM((2, PEERS, SPAN), jnp.int32),
            pltpu.VMEM((2, PEERS, 4 * TOK), F32),
            pltpu.VMEM((2, PEERS, SPAN), F32),
            pltpu.VMEM((PEERS, 4 * TOK), F32),
            pltpu.VMEM((PEERS, SPAN), F32),
            pltpu.VMEM((2 * TOK, HALF), F32),
            pltpu.SemaphoreType.DMA((3,)),
            pltpu.SemaphoreType.DMA((22, PEERS)),
            pltpu.SemaphoreType.DMA((22, PEERS)),
        ],
        compiler_params=pltpu.CompilerParams(
            collective_id=1, has_side_effects=True, vmem_limit_bytes=62 * 1024 * 1024
        ),
        cost_estimate=pl.CostEstimate(flops=18_000_000_000, bytes_accessed=20_000_000, transcendentals=600_000),
        name="moe",
    )(hidden, normed, ids, probs, w_gate, w_up, w_down)


def attn_kernel(
    off_ref, q_hbm, k_hbm, v_hbm, w_hbm, res_hbm, gain_hbm,
    hid_ref, nrm_ref,
    q_ref, res_ref, gain_ref, kv, wbuf, mx, acc, att, pbuf, rbuf, tot, zsnd, zbuf,
    l_sem, kv_s, kv_r, w_s, w_r, y_s, y_r, z_s, z_r,
):
    dp, c, e = lax.axis_index("dp"), lax.axis_index("ctx"), lax.axis_index("exp")
    x, core, y, zh = c // 2, lax.rem(c, 2), e // 2, lax.rem(e, 2)
    sib = 2 * x + 1 - core

    def at_x(i):
        return (dp, 2 * lax.rem(x + i, 4) + core, e)

    def at_y(i):
        return (dp, c, 2 * lax.rem(y + i, 4) + zh)

    at_sib = (dp, sib, e)
    at_z = (dp, c, 2 * y + 1 - zh)

    def rows(ref, index, size):
        return ref.at[pl.ds(pl.multiple_of(index * size, 16), size)]

    def remote(src, dst, s, r, dev):
        return pltpu.make_async_remote_copy(
            src_ref=src, dst_ref=dst, send_sem=s, recv_sem=r, device_id=dev, device_id_type=MESH
        )

    kv_head = lax.rem(y, KVH)
    cols = pl.ds(pl.multiple_of(kv_head * HD, HD), HD)
    own = rows(kv, c, SPAN)
    loads = [
        pltpu.make_async_copy(k_hbm.at[:, cols], own.at[:, :HD], l_sem.at[0]),
        pltpu.make_async_copy(v_hbm.at[:, cols], own.at[:, HD:], l_sem.at[1]),
        pltpu.make_async_copy(w_hbm, rows(wbuf, c, HEADS), l_sem.at[2]),
        pltpu.make_async_copy(q_hbm, q_ref, l_sem.at[3]),
        pltpu.make_async_copy(res_hbm, res_ref, l_sem.at[4]),
        pltpu.make_async_copy(gain_hbm, gain_ref, l_sem.at[5]),
    ]
    for load in loads:
        load.start()
    barrier = pltpu.get_barrier_semaphore()
    peers = [at_x(i) for i in (1, 2, 3)] + [at_y(i) for i in (1, 2, 3)] + [at_sib, at_z]
    for dev in peers:
        pl.semaphore_signal(barrier, 1, device_id=dev, device_id_type=MESH)
    loads[0].wait()
    loads[1].wait()
    pl.semaphore_wait(barrier, len(peers))

    def copies(buf, size, s, r):
        def direct(i):
            return remote(rows(buf, c, size), rows(buf, c, size), s.at[i], r.at[i], at_x(i))

        def arrival(i):
            block = rows(buf, 2 * lax.rem(x + 4 - i, 4) + core, size)
            return remote(block, block, s.at[3 + i], r.at[i], at_sib)

        def handed(i):
            block = rows(buf, 2 * lax.rem(x + 4 - i, 4) + core, size)
            return remote(block, block, s.at[3 + i], r.at[3 + i], at_sib)

        def handed_arrival(i):
            block = rows(buf, 2 * lax.rem(x + 4 - i, 4) + 1 - core, size)
            return remote(block, block, s.at[3 + i], r.at[3 + i], at_sib)

        to_sib = remote(rows(buf, c, size), rows(buf, c, size), s.at[0], r.at[0], at_sib)
        from_sib = remote(rows(buf, sib, size), rows(buf, sib, size), s.at[0], r.at[0], at_sib)
        return direct, arrival, handed, handed_arrival, to_sib, from_sib

    k_direct, k_arrival, k_handed, k_handed_arrival, k_to_sib, k_from_sib = copies(kv, SPAN, kv_s, kv_r)
    w_direct, w_arrival, w_handed, w_handed_arrival, w_to_sib, w_from_sib = copies(wbuf, HEADS, w_s, w_r)
    k_to_sib.start()
    for i in (1, 3, 2):
        k_direct(i).start()

    scale = HD ** (-0.5) * math.log2(math.e)
    lane = lax.broadcasted_iota(jnp.int32, (1, 2 * SPAN), 1)
    ones = jnp.ones((2 * SPAN, HD), BF16)

    def group(i):
        chip = lax.rem(x + 4 - i, 4)
        at = pl.ds(pl.multiple_of(chip * 2 * SPAN, 2 * SPAN), 2 * SPAN)
        first, second = off_ref[2 * chip], off_ref[2 * chip + 1]
        key_pos = jnp.where(lane < SPAN, first + lane, second + lane - SPAN)
        if i:
            bias = jnp.where(key_pos <= off_ref[c] + SPAN - 1, 0.0, NEG_FILL)

        def head(h, _):
            hcols = pl.ds(pl.multiple_of(h * HD, HD), HD)
            mine = pl.ds(pl.multiple_of(h * SPAN, SPAN), SPAN)
            s = lax.dot_general(
                q_ref[:, hcols], kv[at, :HD], (((1,), (1,)), ((), ())), preferred_element_type=F32
            ) * scale
            if i:
                s = s + bias
            else:
                query_pos = off_ref[c] + lax.broadcasted_iota(jnp.int32, (SPAN, 1), 0)
                s = jnp.where(key_pos <= query_pos, s, NEG_FILL)
            top = jnp.max(s, axis=1, keepdims=True)
            if i:
                old = mx[mine, :]
                new = jnp.maximum(old, top)
                p = jnp.exp2(s - jnp.concatenate([new] * 6, axis=1)).astype(BF16)
            else:
                new = jnp.broadcast_to(top, (SPAN, HD))
                p = jnp.exp2(s - top).astype(BF16)
            mixed = jnp.dot(
                p, jnp.concatenate([kv[at, HD:], ones], axis=1), preferred_element_type=F32
            )
            if i:
                keep = jnp.exp2(old - new)
                mixed = acc[mine, :] * jnp.concatenate([keep, keep], axis=1) + mixed
            mx[mine, :] = new
            acc[mine, :] = mixed
            return 0

        lax.fori_loop(0, 8, head, 0)

    loads[2].wait()
    w_to_sib.start()
    for i in (1, 3, 2):
        w_direct(i).start()
    for load in loads[3:]:
        load.wait()
    k_from_sib.wait_recv()
    group(0)
    for i in (1, 3):
        k_arrival(i).wait_recv()
        k_handed(i).start()
    k_handed_arrival(1).wait_recv()
    group(1)
    k_arrival(2).wait_recv()
    k_handed(2).start()
    k_handed_arrival(3).wait_recv()
    group(3)
    k_handed_arrival(2).wait_recv()
    group(2)

    def divide(h, _):
        hcols = pl.ds(pl.multiple_of(h * HD, HD), HD)
        mine = pl.ds(pl.multiple_of(h * SPAN, SPAN), SPAN)
        att[:, hcols] = (acc[mine, :HD] / acc[mine, HD:]).astype(BF16)
        return 0

    lax.fori_loop(0, 8, divide, 0)

    def piece(k):
        k2 = k // 2
        chip = lax.rem(x + 4 - lax.rem(k2 * (k2 + 1) // 2, 4), 4)
        return 2 * chip + lax.rem(core + k, 2)

    def to_y(w, i):
        return remote(
            rows(pbuf, w * 4 + lax.rem(y + i, 4), 2 * TOK), rows(rbuf, w * 3 + i - 1, 2 * TOK),
            y_s.at[w, i - 1], y_r.at[w, i - 1], at_y(i),
        )

    def to_z(w):
        return remote(rows(zsnd, w, TOK), rows(zbuf, w, TOK), z_s.at[w], z_r.at[w], at_z)

    def project(k, _):
        w = piece(k)
        rows(pbuf, w, SPAN)[...] = jnp.dot(
            att[...], rows(wbuf, w, HEADS)[...], preferred_element_type=F32
        ).astype(BF16)
        for i in (1, 3, 2):
            to_y(w, i).start()
        return 0

    def reduce(k, _):
        w = piece(k)
        total = rows(pbuf, w * 4 + y, 2 * TOK)[...].astype(F32)
        for i in (1, 3, 2):
            to_y(w, i).wait_recv()
            total += rows(rbuf, w * 3 + i - 1, 2 * TOK)[...].astype(F32)
        tot[...] = total
        rows(zsnd, w, TOK)[...] = rows(tot, 1 - zh, TOK)[...].astype(BF16)
        to_z(w).start()
        wcols = pl.ds(pl.multiple_of(w * 512, 512), 512)
        hid_ref[:, wcols] = rows(tot, zh, TOK)[...] + res_ref[:, wcols].astype(F32)
        return 0

    w_from_sib.wait_recv()
    lax.fori_loop(0, 2, project, 0)
    for i in (1, 3):
        w_arrival(i).wait_recv()
        w_handed(i).start()
    for i in (1, 3):
        w_handed_arrival(i).wait_recv()
    lax.fori_loop(2, 6, project, 0)
    w_arrival(2).wait_recv()
    w_handed(2).start()
    lax.fori_loop(0, 2, reduce, 0)
    w_handed_arrival(2).wait_recv()
    lax.fori_loop(6, 8, project, 0)
    lax.fori_loop(2, 8, reduce, 0)

    square = jnp.zeros((TOK, 1), F32)

    def finish(k, square):
        w = piece(k)
        to_z(w).wait_recv()
        wcols = pl.ds(pl.multiple_of(w * 512, 512), 512)
        h = hid_ref[:, wcols] + rows(zbuf, w, TOK)[...].astype(F32)
        hid_ref[:, wcols] = h
        return square + jnp.sum(h * h, axis=1, keepdims=True)

    square = lax.fori_loop(0, 8, finish, square)
    inverse = lax.rsqrt(square * (1.0 / D) + 1e-06)
    nrm_ref[...] = (hid_ref[...] * inverse * gain_ref[...]).astype(BF16)

    k_to_sib.wait_send()
    w_to_sib.wait_send()
    for i in (1, 2, 3):
        k_direct(i).wait_send()
        k_handed(i).wait_send()
        w_direct(i).wait_send()
        w_handed(i).wait_send()

    def sent(k, _):
        w = piece(k)
        for i in (1, 2, 3):
            to_y(w, i).wait_send()
        to_z(w).wait_send()
        return 0

    lax.fori_loop(0, 8, sent, 0)


def attend(offsets, queries, keys, values, out_proj, residual, gain):
    vm = pl.BlockSpec(memory_space=pltpu.VMEM)
    hbm = pl.BlockSpec(memory_space=pl.ANY)
    dma = pltpu.SemaphoreType.DMA
    return pl.pallas_call(
        attn_kernel,
        out_shape=(jax.ShapeDtypeStruct((TOK, D), F32), jax.ShapeDtypeStruct((TOK, D), BF16)),
        in_specs=[pl.BlockSpec(memory_space=pltpu.SMEM)] + [hbm] * 6,
        out_specs=(vm, vm),
        scratch_shapes=[
            pltpu.VMEM((SPAN, HEADS), BF16),
            pltpu.VMEM((TOK, D), BF16),
            pltpu.VMEM((1, D), F32),
            pltpu.VMEM((PEERS * SPAN, 2 * HD), BF16),
            pltpu.VMEM((PEERS * HEADS, 512), BF16),
            pltpu.VMEM((8 * SPAN, HD), F32),
            pltpu.VMEM((8 * SPAN, 2 * HD), F32),
            pltpu.VMEM((SPAN, HEADS), BF16),
            pltpu.VMEM((PEERS * SPAN, 512), BF16),
            pltpu.VMEM((PEERS * 3 * 2 * TOK, 512), BF16),
            pltpu.VMEM((2 * TOK, 512), F32),
            pltpu.VMEM((PEERS * TOK, 512), BF16),
            pltpu.VMEM((PEERS * TOK, 512), BF16),
            dma((6,)), dma((7,)), dma((7,)), dma((7,)), dma((7,)),
            dma((PEERS, 3)), dma((PEERS, 3)), dma((PEERS,)), dma((PEERS,)),
        ],
        compiler_params=pltpu.CompilerParams(
            collective_id=2, has_side_effects=True, vmem_limit_bytes=62 * 1024 * 1024
        ),
        cost_estimate=pl.CostEstimate(flops=9_000_000_000, bytes_accessed=4_000_000, transcendentals=10_000_000),
        name="attend",
    )(offsets, queries, keys, values, out_proj, residual, gain)


def shards(
    queries, keys, values, offsets, out_proj, residual, norm_gain, expert_ids, gate_probs, w_gate, w_up, w_down,
):
    hidden, normed = attend(offsets, queries, keys, values, out_proj, residual, norm_gain[None, :])
    return moe(hidden, normed, expert_ids.T, gate_probs.T, w_gate, w_up, w_down)


def solution(mesh):
    return jax.shard_map(
        shards,
        mesh=mesh,
        in_specs=(
            P(("dp", "ctx"), "exp"),
            P(("dp", "ctx"), None),
            P(("dp", "ctx"), None),
            P("dp"),
            P("exp", "ctx"),
            P(("dp", "ctx", "exp"), None),
            P(),
            P(("dp", "ctx", "exp"), None),
            P(("dp", "ctx", "exp"), None),
            P(("ctx", "exp"), None, None),
            P(("ctx", "exp"), None, None),
            P(("ctx", "exp"), None, None),
        ),
        out_specs=P(("dp", "ctx", "exp"), None),
        check_vma=False,
    )
```

time: 248 us -> 211 us (0.85)
  Pallas kernels: 245 us -> 209 us
    pallas_call x1, Pallas kernels: 162 us -> 125 us  [moe(): pl.pallas_call(moe_kernel, out_shape=jax.ShapeDtypeStruct((TOK, D), BF16)...]
where the time goes in v4:
time: 211 us; the launch traced here: 210 us
  Pallas kernels  209 us (99%)
    pallas_call x1, Pallas kernels, moe(): pl.pallas_call(moe_kernel, out_shape=jax.ShapeDtypeStruct((TOK, D), BF16)...  125 us
    pallas_call x1, Pallas kernels, attend(): pl.pallas_call(attn_kernel, out_shape=(jax.ShapeDtypeStruct((TOK, D), F32...  83.8 us

profile of v4, /device:TPU:1, one launch (start us, length us, event | category | flops | bytes accessed | tf_op | source)
XLA Modules:
  0.0 210.4 jit_solution(11698211906755749036)
XLA Ops:
  0.0 83.8 %attend.1 = (f32[48,4096]{1,0:T(8,128)}, bf16[48,4096]{1,0:T(8,128)(2,1)}) custom-call(s32[8]{0:T(128)} %off_ref.1, bf16[384,1024]{1,0:T(8,128)(2,1)} %q_hbm.1, bf16[384,512]{1,0:T(8,128)(2,1)} %k_hbm.1, bf16[384,512]{1,0:T(8,128)(2,1)} %v_hbm.1, bf16[1024,512]{1,0:T(8,128)(2,1)} %w_hbm.1, bf16[48,4096]{1,0:T(8,128)(2,1)} %res_hbm.1, f32[1,4096]{1,0:T(1,128)} %bitcast.3), custom_call_target="tpu_custom_call" | custom-call | flops 8999999488 | bytes 4000000 | tf_op jit(solution)/shard_map/attend/pallas_call | solution.py:691
  83.8 124.8 %moe.1 = bf16[48,4096]{1,0:T(8,128)(2,1)} custom-call(f32[48,4096]{1,0:T(8,128)} %get-tuple-element.7.hid_ref, bf16[48,4096]{1,0:T(8,128)(2,1)} %get-tuple-element.8.nrm_ref, s32[8,48]{1,0:T(8,128)} %bitcast.4, f32[8,48]{1,0:T(8,128)} %bitcast.5, bf16[1,4096,768]{2,1,0:T(8,128)(2,1)} %wg_hbm.1, bf16[1,4096,768]{2,1,0:T(8,128)(2,1)} %wu_hbm.1, ...), custom_call_target="tpu_custom_call" | custom-call | flops 17999998976 | bytes 20000000 | tf_op jit(solution)/shard_map/moe/pallas_call | solution.py:424
  208.6 1.8 copy.14

commit v5 on v4

--- a/solution.py
+++ b/solution.py
@@ -474,6 +474,7 @@
 
     at_sib = (dp, sib, e)
     at_z = (dp, c, 2 * y + 1 - zh)
+    at_twin = (1 - dp, c, e)
 
     def rows(ref, index, size):
         return ref.at[pl.ds(pl.multiple_of(index * size, 16), size)]
@@ -497,35 +498,45 @@
     for load in loads:
         load.start()
     barrier = pltpu.get_barrier_semaphore()
-    peers = [at_x(i) for i in (1, 2, 3)] + [at_y(i) for i in (1, 2, 3)] + [at_sib, at_z]
+    peers = [at_x(i) for i in (1, 2, 3)] + [at_y(i) for i in (1, 2, 3)] + [at_sib, at_z, at_twin]
     for dev in peers:
         pl.semaphore_signal(barrier, 1, device_id=dev, device_id_type=MESH)
     loads[0].wait()
     loads[1].wait()
     pl.semaphore_wait(barrier, len(peers))
 
-    def copies(buf, size, s, r):
-        def direct(i):
-            return remote(rows(buf, c, size), rows(buf, c, size), s.at[i], r.at[i], at_x(i))
-
-        def arrival(i):
-            block = rows(buf, 2 * lax.rem(x + 4 - i, 4) + core, size)
-            return remote(block, block, s.at[3 + i], r.at[i], at_sib)
-
-        def handed(i):
-            block = rows(buf, 2 * lax.rem(x + 4 - i, 4) + core, size)
+    def from_chip(buf, size, i, who):
+        return rows(buf, 2 * lax.rem(x + 4 - i, 4) + who, size)
+
+    def exchange(buf, size, s, r):
+        def handed(i, who):
+            block = from_chip(buf, size, i, who)
             return remote(block, block, s.at[3 + i], r.at[3 + i], at_sib)
 
-        def handed_arrival(i):
-            block = rows(buf, 2 * lax.rem(x + 4 - i, 4) + 1 - core, size)
-            return remote(block, block, s.at[3 + i], r.at[3 + i], at_sib)
-
-        to_sib = remote(rows(buf, c, size), rows(buf, c, size), s.at[0], r.at[0], at_sib)
-        from_sib = remote(rows(buf, sib, size), rows(buf, sib, size), s.at[0], r.at[0], at_sib)
-        return direct, arrival, handed, handed_arrival, to_sib, from_sib
-
-    k_direct, k_arrival, k_handed, k_handed_arrival, k_to_sib, k_from_sib = copies(kv, SPAN, kv_s, kv_r)
-    w_direct, w_arrival, w_handed, w_handed_arrival, w_to_sib, w_from_sib = copies(wbuf, HEADS, w_s, w_r)
+        mine, theirs = rows(buf, c, size), rows(buf, sib, size)
+        to_sib = remote(mine, mine, s.at[0], r.at[0], at_sib)
+        from_sib = remote(theirs, theirs, s.at[0], r.at[0], at_sib)
+        return handed, to_sib, from_sib
+
+    k_handed, k_to_sib, k_from_sib = exchange(kv, SPAN, kv_s, kv_r)
+    w_handed, w_to_sib, w_from_sib = exchange(wbuf, HEADS, w_s, w_r)
+
+    def k_direct(i):
+        return remote(own, own, kv_s.at[i], kv_r.at[i], at_x(i))
+
+    def k_arrival(i):
+        block = from_chip(kv, SPAN, i, core)
+        return remote(block, block, kv_s.at[i], kv_r.at[i], at_sib)
+
+    def w_direct(i, coming):
+        block = from_chip(wbuf, HEADS, i, core) if coming else rows(wbuf, c, HEADS)
+        part = rows(block, dp, 512) if i == 2 else block
+        return remote(part, part, w_s.at[i], w_r.at[i], at_x(i))
+
+    def w_twin(coming):
+        part = rows(from_chip(wbuf, HEADS, 2, core), 1 - dp if coming else dp, 512)
+        return remote(part, part, w_s.at[7], w_r.at[7], at_twin)
+
     k_to_sib.start()
     for i in (1, 3, 2):
         k_direct(i).start()
@@ -571,26 +582,29 @@
             acc[mine, :] = mixed
             return 0
 
-        lax.fori_loop(0, 8, head, 0)
+        lax.fori_loop(0, 8, head, 0, unroll=8)
 
     loads[2].wait()
     w_to_sib.start()
-    for i in (1, 3, 2):
-        w_direct(i).start()
+    w_direct(2, False).start()
     for load in loads[3:]:
         load.wait()
     k_from_sib.wait_recv()
     group(0)
+    w_direct(1, False).start()
+    w_direct(3, False).start()
     for i in (1, 3):
         k_arrival(i).wait_recv()
-        k_handed(i).start()
-    k_handed_arrival(1).wait_recv()
+        k_handed(i, core).start()
+    k_handed(1, 1 - core).wait_recv()
     group(1)
     k_arrival(2).wait_recv()
-    k_handed(2).start()
-    k_handed_arrival(3).wait_recv()
+    k_handed(2, core).start()
+    k_handed(3, 1 - core).wait_recv()
     group(3)
-    k_handed_arrival(2).wait_recv()
+    k_handed(2, 1 - core).wait_recv()
+    w_direct(2, True).wait_recv()
+    w_twin(False).start()
     group(2)
 
     def divide(h, _):
@@ -603,7 +617,7 @@
 
     def piece(k):
         k2 = k // 2
-        chip = lax.rem(x + 4 - lax.rem(k2 * (k2 + 1) // 2, 4), 4)
+        chip = lax.rem(x + 4 - lax.rem(2 * k2, 4) - k2 // 2, 4)
         return 2 * chip + lax.rem(core + k, 2)
 
     def to_y(w, i):
@@ -639,18 +653,23 @@
 
     w_from_sib.wait_recv()
     lax.fori_loop(0, 2, project, 0)
+    w_twin(True).wait_recv()
+    w_handed(2, core).start()
+    project(2, 0)
+    lax.fori_loop(0, 2, reduce, 0)
+    w_handed(2, 1 - core).wait_recv()
+    project(3, 0)
     for i in (1, 3):
-        w_arrival(i).wait_recv()
-        w_handed(i).start()
+        w_direct(i, True).wait_recv()
+        w_handed(i, core).start()
+    lax.fori_loop(0, 2, lambda j, _: project(4 + 2 * j, 0), 0)
     for i in (1, 3):
-        w_handed_arrival(i).wait_recv()
-    lax.fori_loop(2, 6, project, 0)
-    w_arrival(2).wait_recv()
-    w_handed(2).start()
-    lax.fori_loop(0, 2, reduce, 0)
-    w_handed_arrival(2).wait_recv()
-    lax.fori_loop(6, 8, project, 0)
-    lax.fori_loop(2, 8, reduce, 0)
+        w_handed(i, 1 - core).wait_recv()
+    lax.fori_loop(0, 2, lambda j, _: project(5 + 2 * j, 0), 0)
+    lax.fori_loop(2, 5, reduce, 0)
+    reduce(6, 0)
+    reduce(5, 0)
+    reduce(7, 0)
 
     square = jnp.zeros((TOK, 1), F32)
 
@@ -670,9 +689,10 @@
     w_to_sib.wait_send()
     for i in (1, 2, 3):
         k_direct(i).wait_send()
-        k_handed(i).wait_send()
-        w_direct(i).wait_send()
-        w_handed(i).wait_send()
+        k_handed(i, core).wait_send()
+        w_direct(i, False).wait_send()
+        w_handed(i, core).wait_send()
+    w_twin(False).wait_send()
 
     def sent(k, _):
         w = piece(k)
@@ -707,7 +727,7 @@
             pltpu.VMEM((2 * TOK, 512), F32),
             pltpu.VMEM((PEERS * TOK, 512), BF16),
             pltpu.VMEM((PEERS * TOK, 512), BF16),
-            dma((6,)), dma((7,)), dma((7,)), dma((7,)), dma((7,)),
+            dma((6,)), dma((7,)), dma((7,)), dma((8,)), dma((8,)),
             dma((PEERS, 3)), dma((PEERS, 3)), dma((PEERS,)), dma((PEERS,)),
         ],
         compiler_params=pltpu.CompilerParams(

time: 211 us -> 206 us (0.976)
  Pallas kernels: 209 us -> 204 us
    pallas_call x1, Pallas kernels: 83.8 us -> 77.4 us  [attend(): pl.pallas_call(attn_kernel, out_shape=(jax.ShapeDtypeStruct((TOK, D), F32...]
where the time goes in v5:
time: 206 us
  Pallas kernels  204 us (99%)
    pallas_call x1, Pallas kernels, moe(): pl.pallas_call(moe_kernel, out_shape=jax.ShapeDtypeStruct((TOK, D), BF16)...  127 us
    pallas_call x1, Pallas kernels, attend(): pl.pallas_call(attn_kernel, out_shape=(jax.ShapeDtypeStruct((TOK, D), F32...  77.4 us

profile of v5, /device:TPU:1, one launch (start us, length us, event | category | flops | bytes accessed | tf_op | source)
XLA Modules:
  0.0 206.0 jit_solution(10280616658057628384)
XLA Ops:
  0.0 77.4 %attend.1 = (f32[48,4096]{1,0:T(8,128)}, bf16[48,4096]{1,0:T(8,128)(2,1)}) custom-call(s32[8]{0:T(128)} %off_ref.1, bf16[384,1024]{1,0:T(8,128)(2,1)} %q_hbm.1, bf16[384,512]{1,0:T(8,128)(2,1)} %k_hbm.1, bf16[384,512]{1,0:T(8,128)(2,1)} %v_hbm.1, bf16[1024,512]{1,0:T(8,128)(2,1)} %w_hbm.1, bf16[48,4096]{1,0:T(8,128)(2,1)} %res_hbm.1, f32[1,4096]{1,0:T(1,128)} %bitcast.3), custom_call_target="tpu_custom_call" | custom-call | flops 8999999488 | bytes 4000000 | tf_op jit(solution)/shard_map/attend/pallas_call | solution.py:711
  77.4 126.9 %moe.1 = bf16[48,4096]{1,0:T(8,128)(2,1)} custom-call(f32[48,4096]{1,0:T(8,128)} %get-tuple-element.7.hid_ref, bf16[48,4096]{1,0:T(8,128)(2,1)} %get-tuple-element.8.nrm_ref, s32[8,48]{1,0:T(8,128)} %bitcast.4, f32[8,48]{1,0:T(8,128)} %bitcast.5, bf16[1,4096,768]{2,1,0:T(8,128)(2,1)} %wg_hbm.1, bf16[1,4096,768]{2,1,0:T(8,128)(2,1)} %wu_hbm.1, ...), custom_call_target="tpu_custom_call" | custom-call | flops 17999998976 | bytes 20000000 | tf_op jit(solution)/shard_map/moe/pallas_call | solution.py:424
  204.3 1.8 copy.14

commit v6 on v5

--- a/solution.py
+++ b/solution.py
@@ -626,6 +626,25 @@
             y_s.at[w, i - 1], y_r.at[w, i - 1], at_y(i),
         )
 
+    def by_way(w, k):
+        wide = slice(k * 256, k * 256 + 256)
+        return remote(
+            rows(pbuf, w * 4 + lax.rem(y + 2, 4), 2 * TOK).at[:, wide], rows(rbuf, w * 3 + 1, 2 * TOK).at[:, wide],
+            y_s.at[w, 1 + 2 * k], y_r.at[w, 1 + 2 * k], at_y(1 + 2 * k),
+        )
+
+    def relay(k, _):
+        w = piece(k)
+        for h in range(2):
+            wide = slice(h * 256, h * 256 + 256)
+            by_way(w, h).wait_recv()
+            block = rows(pbuf, w * 4 + lax.rem(y + 1 + 2 * h, 4), 2 * TOK)
+            block[:, wide] = (
+                block[:, wide].astype(F32) + rows(rbuf, w * 3 + 1, 2 * TOK)[:, wide].astype(F32)
+            ).astype(BF16)
+            to_y(w, 1 + 2 * h).start()
+        return 0
+
     def to_z(w):
         return remote(rows(zsnd, w, TOK), rows(zbuf, w, TOK), z_s.at[w], z_r.at[w], at_z)
 
@@ -634,14 +653,14 @@
         rows(pbuf, w, SPAN)[...] = jnp.dot(
             att[...], rows(wbuf, w, HEADS)[...], preferred_element_type=F32
         ).astype(BF16)
-        for i in (1, 3, 2):
-            to_y(w, i).start()
+        for h in range(2):
+            by_way(w, h).start()
         return 0
 
     def reduce(k, _):
         w = piece(k)
         total = rows(pbuf, w * 4 + y, 2 * TOK)[...].astype(F32)
-        for i in (1, 3, 2):
+        for i in (1, 3):
             to_y(w, i).wait_recv()
             total += rows(rbuf, w * 3 + i - 1, 2 * TOK)[...].astype(F32)
         tot[...] = total
@@ -653,12 +672,14 @@
 
     w_from_sib.wait_recv()
     lax.fori_loop(0, 2, project, 0)
+    lax.fori_loop(0, 2, relay, 0)
     w_twin(True).wait_recv()
     w_handed(2, core).start()
     project(2, 0)
     lax.fori_loop(0, 2, reduce, 0)
     w_handed(2, 1 - core).wait_recv()
     project(3, 0)
+    lax.fori_loop(2, 4, relay, 0)
     for i in (1, 3):
         w_direct(i, True).wait_recv()
         w_handed(i, core).start()
@@ -666,10 +687,8 @@
     for i in (1, 3):
         w_handed(i, 1 - core).wait_recv()
     lax.fori_loop(0, 2, lambda j, _: project(5 + 2 * j, 0), 0)
-    lax.fori_loop(2, 5, reduce, 0)
-    reduce(6, 0)
-    reduce(5, 0)
-    reduce(7, 0)
+    lax.fori_loop(4, 8, relay, 0)
+    lax.fori_loop(2, 8, reduce, 0)
 
     square = jnp.zeros((TOK, 1), F32)
 
@@ -696,8 +715,9 @@
 
     def sent(k, _):
         w = piece(k)
-        for i in (1, 2, 3):
-            to_y(w, i).wait_send()
+        for h in range(2):
+            by_way(w, h).wait_send()
+            to_y(w, 1 + 2 * h).wait_send()
         to_z(w).wait_send()
         return 0
 
@@ -728,7 +748,7 @@
             pltpu.VMEM((PEERS * TOK, 512), BF16),
             pltpu.VMEM((PEERS * TOK, 512), BF16),
             dma((6,)), dma((7,)), dma((7,)), dma((8,)), dma((8,)),
-            dma((PEERS, 3)), dma((PEERS, 3)), dma((PEERS,)), dma((PEERS,)),
+            dma((PEERS, 4)), dma((PEERS, 4)), dma((PEERS,)), dma((PEERS,)),
         ],
         compiler_params=pltpu.CompilerParams(
             collective_id=2, has_side_effects=True, vmem_limit_bytes=62 * 1024 * 1024

time: 206 us -> 204 us (level)
    pallas_call x1, Pallas kernels: 77.4 us -> 75.2 us  [attend(): pl.pallas_call(attn_kernel, out_shape=(jax.ShapeDtypeStruct((TOK, D), F32...]
where the time goes in v6:
time: 204 us
  Pallas kernels  202 us (99%)
    pallas_call x1, Pallas kernels, moe(): pl.pallas_call(moe_kernel, out_shape=jax.ShapeDtypeStruct((TOK, D), BF16)...  127 us
    pallas_call x1, Pallas kernels, attend(): pl.pallas_call(attn_kernel, out_shape=(jax.ShapeDtypeStruct((TOK, D), F32...  75.2 us

profile of v6, /device:TPU:1, one launch (start us, length us, event | category | flops | bytes accessed | tf_op | source)
XLA Modules:
  0.0 203.7 jit_solution(8441854343564118043)
XLA Ops:
  0.0 75.2 %attend.1 = (f32[48,4096]{1,0:T(8,128)}, bf16[48,4096]{1,0:T(8,128)(2,1)}) custom-call(s32[8]{0:T(128)} %off_ref.1, bf16[384,1024]{1,0:T(8,128)(2,1)} %q_hbm.1, bf16[384,512]{1,0:T(8,128)(2,1)} %k_hbm.1, bf16[384,512]{1,0:T(8,128)(2,1)} %v_hbm.1, bf16[1024,512]{1,0:T(8,128)(2,1)} %w_hbm.1, bf16[48,4096]{1,0:T(8,128)(2,1)} %res_hbm.1, f32[1,4096]{1,0:T(1,128)} %bitcast.3), custom_call_target="tpu_custom_call" | custom-call | flops 8999999488 | bytes 4000000 | tf_op jit(solution)/shard_map/attend/pallas_call | solution.py:731
  75.2 126.8 %moe.1 = bf16[48,4096]{1,0:T(8,128)(2,1)} custom-call(f32[48,4096]{1,0:T(8,128)} %get-tuple-element.7.hid_ref, bf16[48,4096]{1,0:T(8,128)(2,1)} %get-tuple-element.8.nrm_ref, s32[8,48]{1,0:T(8,128)} %bitcast.4, f32[8,48]{1,0:T(8,128)} %bitcast.5, bf16[1,4096,768]{2,1,0:T(8,128)(2,1)} %wg_hbm.1, bf16[1,4096,768]{2,1,0:T(8,128)(2,1)} %wu_hbm.1, ...), custom_call_target="tpu_custom_call" | custom-call | flops 17999998976 | bytes 20000000 | tf_op jit(solution)/shard_map/moe/pallas_call | solution.py:424
  202.0 1.8 copy.14
